TPU v7x, 256 devices: a whole 4x4x8 slice. The times are simulated.
256 devices in a mesh: fluid: 4 (over y), sx: 8 (over z), sy: 8 (over x, core).
Axes of the slice: x: 4, y: 4, z: 8, core: 2. Of those that a mesh axis runs over, the one named last changes fastest.
Arguments:
- opening_conductor_warmth: float32 [128, 128, 512], P('sx', 'sy', 'fluid'), may hold values from -19 to 19
- cellwise_diffusivity: float32 [128, 128, 512], P('sx', 'sy', 'fluid'), may hold values from 0.15 to 1
- previous_thermal_states: float32 [56, 128, 128, 512], P(None, 'sx', 'sy', 'fluid'), may hold values from -19 to 19
- boundary_heat_rate_pieces: float32 [1048576, 128], P(('fluid', 'sx', 'sy')), may hold values from -6 to 6
- receiving_processor_per_piece: int32 [1048576, 1], P(('fluid', 'sx', 'sy')), may hold values from 0 to 255; in each aligned block of 4096 rows (0 to 4095, 4096 to 8191, ...) at most 32 rows name the same one
- boundary_line_position_in_tile: int32 [1048576, 1], P(('fluid', 'sx', 'sy')), may hold values from 0 to 255
- piece_to_solid_line_mapping: float32 [128, 128], replicated, may hold values from -0.5 to 0.5
Outputs:
- field_out: float32 [128, 128, 512], P('sx', 'sy', 'fluid')
- inner_product_matrix: float32 [64, 64], P(('sx', 'sy'))
Inputs may be any that keep to these rules, and one draw needn't show every extreme that they name: `receiving_processor_per_piece`: among one device's 4096 rows no device is named more than 32 times, and in every draw some device is named exactly 32 times by one device's rows.
All inputs are finite; a program needn't handle non-finite values.
Results may differ from a plain program's by a relative error of at most 0.000088.
Values sent between devices are 32-bit elements; how exact they have to be, the bound alone decides.
No kernel may reach another device: no remote copies, remote signals or barrier semaphores. Data moves between devices by JAX's collectives and lax.ppermute only.
A program may use at most 128 MiB of HBM per device.

v0:
```python
import jax
import jax.numpy as jnp
from jax import lax
from jax.sharding import PartitionSpec as P

STEPS = 8


rate_step = 0.16
source_gain = 0.1


def extended(cells, sides, width):
    for axis, dim in sides:
        count = lax.axis_size(axis)
        ends = count - 1
        head = lax.slice_in_dim(cells, 0, width, axis=dim)
        tail = lax.slice_in_dim(cells, cells.shape[dim] - width, cells.shape[dim], axis=dim)
        cells = jnp.concatenate(
            [
                lax.ppermute(tail, axis, [(i, (i + 1) % count) for i in range(ends)]),
                cells,
                lax.ppermute(head, axis, [((i + 1) % count, i) for i in range(ends)]),
            ],
            axis=dim,
        )
    return cells


def increment_change(margin_extended_grid, cellwise_diffusivity, deposited_energy):
    center = margin_extended_grid[1:-1, 1:-1, 1:-1]
    beside = margin_extended_grid[2:, 1:-1, 1:-1] + margin_extended_grid[:-2, 1:-1, 1:-1]
    beside = beside + margin_extended_grid[1:-1, 2:, 1:-1] + margin_extended_grid[1:-1, :-2, 1:-1]
    beside = beside + margin_extended_grid[1:-1, 1:-1, 2:] + margin_extended_grid[1:-1, 1:-1, :-2]
    return center + rate_step * cellwise_diffusivity * (beside - 6.0 * center) + deposited_energy


def map_lines(blocks, piece_to_solid_line_mapping):
    return jnp.dot(
        blocks,
        piece_to_solid_line_mapping,
        precision=lax.Precision.HIGHEST,
        preferred_element_type=jnp.float32,
    )


def local(
    opening_conductor_warmth,
    cellwise_diffusivity,
    previous_thermal_states,
    boundary_heat_rate_pieces,
    receiving_processor_per_piece,
    boundary_line_position_in_tile,
    piece_to_solid_line_mapping,
):
    count_fluid = lax.axis_size("fluid")
    count_tiles = lax.axis_size("sx") * lax.axis_size("sy")
    count_all = count_fluid * count_tiles
    block_count = boundary_heat_rate_pieces.shape[0]
    capacity = 2 * block_count // count_all
    solid_thickness_horizontal, solid_thickness_vertical, solid_thickness_normal = (
        opening_conductor_warmth.shape
    )
    target = receiving_processor_per_piece[:, 0]
    matches = (target[:, None] == jnp.arange(count_all, dtype=jnp.int32)[None, :]).astype(jnp.int32)
    order_rank = jnp.sum(jnp.cumsum(matches, axis=0) * matches, axis=1) - 1
    slot_index = target * capacity + order_rank
    buffer = (
        jnp.zeros((count_all * capacity, boundary_heat_rate_pieces.shape[1]), jnp.float32)
        .at[slot_index]
        .set(boundary_heat_rate_pieces)
    )
    labels_out = (
        jnp.full((count_all * capacity,), -1.0, jnp.float32)
        .at[slot_index]
        .set(boundary_line_position_in_tile[:, 0].astype(jnp.float32))
    )
    buffer = buffer.reshape(count_fluid, count_tiles, capacity, boundary_heat_rate_pieces.shape[1])
    labels_out = labels_out.reshape(count_fluid, count_tiles, capacity)
    received, labels = (
        lax.all_to_all(
            lax.all_to_all(buffer, "fluid", split_axis=0, concat_axis=0, tiled=True),
            ("sx", "sy"),
            split_axis=1,
            concat_axis=1,
            tiled=True,
        ),
        lax.all_to_all(
            lax.all_to_all(labels_out, "fluid", split_axis=0, concat_axis=0, tiled=True),
            ("sx", "sy"),
            split_axis=1,
            concat_axis=1,
            tiled=True,
        ),
    )
    received = received.reshape(count_all * capacity, boundary_heat_rate_pieces.shape[1])
    labels = labels.reshape(count_all * capacity)
    received = map_lines(received, piece_to_solid_line_mapping)
    onehot = (
        jnp.arange(solid_thickness_horizontal * solid_thickness_vertical, dtype=jnp.float32)[
            :, None
        ]
        == labels[None, :]
    ).astype(jnp.float32)
    deposit = jnp.dot(
        onehot, received, precision=lax.Precision.HIGHEST, preferred_element_type=jnp.float32
    )
    deposited_energy = source_gain * deposit.reshape(
        solid_thickness_horizontal, solid_thickness_vertical, solid_thickness_normal
    )
    existing_conductor_warmth = opening_conductor_warmth
    recorded_frames = []
    for step_index in range(STEPS):
        margin_extended_grid = extended(
            existing_conductor_warmth, (("fluid", 2), ("sx", 0), ("sy", 1)), 1
        )
        existing_conductor_warmth = increment_change(
            margin_extended_grid, cellwise_diffusivity, deposited_energy
        )
        recorded_frames.append(existing_conductor_warmth)
    cells = float(
        solid_thickness_horizontal * solid_thickness_vertical * solid_thickness_normal * count_all
    )
    gathered_snapshots = jnp.concatenate(
        [
            previous_thermal_states.reshape(previous_thermal_states.shape[0], -1),
            jnp.stack(recorded_frames).reshape(len(recorded_frames), -1),
        ],
        0,
    )
    local_gram = (
        jnp.dot(
            gathered_snapshots,
            gathered_snapshots.T,
            precision=lax.Precision.HIGHEST,
            preferred_element_type=jnp.float32,
        )
        / cells
    )
    owned_rows = lax.psum_scatter(local_gram, ("sx", "sy"), scatter_dimension=0, tiled=True)
    inner_product_matrix = lax.psum(owned_rows, "fluid")
    return (existing_conductor_warmth, inner_product_matrix)


def solution(mesh):
    placed = (
        P("sx", "sy", "fluid"),
        P("sx", "sy", "fluid"),
        P(None, "sx", "sy", "fluid"),
        P(("fluid", "sx", "sy"), None),
        P(("fluid", "sx", "sy"), None),
        P(("fluid", "sx", "sy"), None),
        P(),
    )
    return jax.shard_map(
        local,
        mesh=mesh,
        in_specs=placed,
        out_specs=(P("sx", "sy", "fluid"), P(("sx", "sy"), None)),
        check_vma=False,
    )
```

profile of v0, /device:TPU:1, one launch (start us, length us, event | category | flops | bytes accessed | tf_op | source)
XLA Modules:
  0.0 706.1 jit_solution(9592213935619952687)
XLA Ops:
  10.9 15.5 %scatter_custom_fusion = f32[8192]{0:T(1024)S(1)} fusion(s32[4096]{0:T(1024)S(1)} %bitcast.68, f32[4096]{0:T(1024)S(1)} %bitcast.70, f32[]{:T(128)} %constant.5.clone.1), kind=kCustom, calls=%fused_computation.300 | custom fusion | bytes 32772 | tf_op jit(solution)/shard_map/scatter | solution.py:76
  27.4 5.0 all-to-all-start
  32.4 13.1 %scatter_custom_fusion.1 = f32[8192,128]{1,0:T(8,128)} fusion(s32[4096]{0:T(1024)S(1)} %bitcast.69, f32[4096,128]{1,0:T(8,128)} %param.10, f32[]{:T(128)} %constant.24.clone.1), kind=kCustom, calls=%fused_computation.12 | custom fusion | bytes 4194816 | tf_op jit(solution)/shard_map/scatter | solution.py:71
  45.5 4.9 all-to-all-start.2
  52.6 45.2 %all-to-all-done.2 = f32[4,64,32,128]{3,2,1,0:T(8,128)} async-done(((f32[4,64,32,128]{3,2,1,0:T(8,128)}), f32[4,64,32,128]{3,2,1,0:T(8,128)}, u32[]{:S(2)}, u32[]{:S(2)}) %all-to-all-start.2) | async-done | bytes 4194336 | tf_op jit(solution)/shard_map/all_to_all | solution.py:82
  97.8 13.9 %all-to-all-start.1 = ((f32[64,1,128]{2,1,0:T(1,128)}), f32[64,1,128]{2,1,0:T(1,128)S(1)}, u32[]{:S(2)}, u32[]{:S(2)}) async-start(f32[64,1,128]{2,1,0:T(1,128)} %reshape.91), calls=%async_computation.1 | async-start | bytes 65536 | tf_op jit(solution)/shard_map/all_to_all | solution.py:88
  111.7 4.8 copy.30
  116.6 4.5 all-to-all-done.1
  121.0 6.2 all-to-all-start.3
  137.1 4.1 collective-permute-start.3
  141.2 77.0 %collective-permute-done.2 = f32[1,16,130]{2,1,0:T(8,128)S(1)} collective-permute-done((f32[1,16,130]{2,1,0:T(8,128)S(1)}, f32[1,16,130]{2,1,0:T(8,128)S(1)}, u32[]{:S(2)}, u32[]{:S(2)}) %collective-permute-start.2) | collective-permute-done | bytes 8352 | tf_op jit(solution)/shard_map/ppermute | solution.py:23
  231.8 4.2 fusion.8
  252.1 4.1 collective-permute-start.10
  264.7 4.7 collective-permute-done.13
  270.9 4.5 collective-permute-start.15
  290.7 4.1 collective-permute-done.19
  296.2 4.7 collective-permute-start.21
  305.0 4.4 collective-permute-start.23
  314.3 4.1 collective-permute-done.25
  319.7 5.5 collective-permute-start.27
  328.4 6.5 collective-permute-start.29
  344.9 5.8 collective-permute-start.33
  353.6 6.5 collective-permute-start.35
  370.2 5.8 collective-permute-start.39
  378.9 6.5 collective-permute-start.41
  395.5 5.8 collective-permute-start.45
  404.2 6.5 collective-permute-start.47
  410.7 7.0 copy.34
  418.7 19.5 %concatenate.269 = f32[64,32768]{1,0:T(8,128)} concatenate(f32[56,32768]{1,0:T(8,128)} %bitcast.40, f32[1,32768]{1,0:T(1,128)S(1)} %bitcast.53, f32[1,32768]{1,0:T(1,128)S(1)} %bitcast.54, f32[1,32768]{1,0:T(1,128)S(1)} %bitcast.55, f32[1,32768]{1,0:T(1,128)S(1)} %bitcast.56, f32[1,32768]{1,0:T(1,128)S(1)} %bitcast.57, f32[1,32768]{1,0:T(1,128)S(1)} %bitcast.58, ...), dimensions={0} | concatenate | bytes 16777216 | tf_op jit(solution)/shard_map/concatenate | solution.py:124
  438.2 10.5 %convolution_multiply_fusion = f32[64,64]{1,0:T(8,128)S(1)} fusion(f32[64,32768]{1,0:T(8,128)} %concatenate.269), kind=kOutput, calls=%fused_computation.17 | convolution fusion | flops 1610616832 | bytes 8404992 | tf_op jit(solution)/shard_map/dot_general | solution.py:132
  448.7 250.3 %all-reduce = f32[64,64]{1,0:T(8,128)S(1)} all-reduce(f32[64,64]{1,0:T(8,128)S(1)} %convolution_multiply_fusion), channel_id=2, replica_groups=mesh['fluid'=4,'sx'=8,'sy'=8] {'sx','sy'}, use_global_device_ids=true, to_apply=%region_5.6.clone | all-reduce | flops 4096 | bytes 32768
  699.6 6.5 psum.7
  (163 shorter events, 133.0 us)
Async XLA Ops:
  27.4 18.2 %all-to-all-start = ((f32[4,1,2048]{2,1,0:T(1,128)}), f32[4,1,2048]{2,1,0:T(1,128)S(1)}, u32[]{:S(2)}, u32[]{:S(2)}) async-start(f32[4,1,2048]{2,1,0:T(1,128)} %reshape.89), calls=%async_computation | async-start | bytes 65536 | tf_op jit(solution)/shard_map/all_to_all | solution.py:89
  45.5 52.3 %all-to-all-start.2 = ((f32[4,64,32,128]{3,2,1,0:T(8,128)}), f32[4,64,32,128]{3,2,1,0:T(8,128)}, u32[]{:S(2)}, u32[]{:S(2)}) async-start(f32[4,64,32,128]{3,2,1,0:T(8,128)} %bitcast.41), calls=%async_computation.2 | async-start | bytes 8388608 | tf_op jit(solution)/shard_map/all_to_all | solution.py:82
  97.8 23.2 %all-to-all-start.1 = ((f32[64,1,128]{2,1,0:T(1,128)}), f32[64,1,128]{2,1,0:T(1,128)S(1)}, u32[]{:S(2)}, u32[]{:S(2)}) async-start(f32[64,1,128]{2,1,0:T(1,128)} %reshape.91), calls=%async_computation.1 | async-start | bytes 65536 | tf_op jit(solution)/shard_map/all_to_all | solution.py:88
  121.0 104.4 %all-to-all-start.3 = ((f32[4,64,32,128]{3,2,0,1:T(8,128)}), f32[4,64,32,128]{3,2,0,1:T(8,128)}, u32[]{:S(2)}, u32[]{:S(2)}) async-start(f32[4,64,32,128]{3,2,0,1:T(8,128)} %copy.30), calls=%async_computation.3 | async-start | bytes 8388608 | tf_op jit(solution)/shard_map/all_to_all | solution.py:81
  129.5 6.2 collective-permute-start.1
  135.8 82.4 %collective-permute-start.2 = (f32[1,16,130]{2,1,0:T(8,128)S(1)}, f32[1,16,130]{2,1,0:T(8,128)S(1)}, u32[]{:S(2)}, u32[]{:S(2)}) collective-permute-start(f32[1,16,130]{2,1,0:T(8,128)S(1)} %get-tuple-element.33), channel_id=1, source_target_pairs={{8,0},{16,8},{24,16},{32,24},{40,32},{48,40},{56,48},{9,1},{17,9},... | collective-permute-start | bytes 24968 | tf_op jit(solution)/shard_map/ppermute | solution.py:23
  137.1 81.1 %collective-permute-start.3 = (f32[1,16,130]{2,1,0:T(8,128)S(1)}, f32[1,16,130]{2,1,0:T(8,128)S(1)}, u32[]{:S(2)}, u32[]{:S(2)}) collective-permute-start(f32[1,16,130]{2,1,0:T(8,128)S(1)} %get-tuple-element.32), channel_id=1, source_target_pairs={{0,8},{8,16},{16,24},{24,32},{32,40},{40,48},{48,56},{1,9},{9,17},... | collective-permute-start | bytes 24968 | tf_op jit(solution)/shard_map/ppermute | solution.py:21
  218.4 17.6 %collective-permute-start.4 = (f32[18,1,130]{2,1,0:T(1,128)S(1)}, f32[18,1,130]{2,1,0:T(1,128)S(1)}, u32[]{:S(2)}, u32[]{:S(2)}) collective-permute-start(f32[18,1,130]{2,1,0:T(1,128)S(1)} %get-tuple-element.16), channel_id=1, source_target_pairs={{1,0},{2,1},{3,2},{4,3},{5,4},{6,5},{7,6},{9,8},{10,9},{11,10},{12... | collective-permute-start | bytes 28088 | tf_op jit(solution)/shard_map/ppermute | solution.py:23
  221.8 14.2 %collective-permute-start.5 = (f32[18,1,130]{2,1,0:T(1,128)S(1)}, f32[18,1,130]{2,1,0:T(1,128)S(1)}, u32[]{:S(2)}, u32[]{:S(2)}) collective-permute-start(f32[18,1,130]{2,1,0:T(1,128)S(1)} %get-tuple-element.17), channel_id=1, source_target_pairs={{0,1},{1,2},{2,3},{3,4},{4,5},{5,6},{6,7},{8,9},{9,10},{10,11},{11... | collective-permute-start | bytes 28088 | tf_op jit(solution)/shard_map/ppermute | solution.py:21
  239.0 6.8 collective-permute-start.7
  252.1 6.9 collective-permute-start.10
  261.8 7.6 %collective-permute-start.13 = (f32[16,16,1]{2,1,0:T(8,128)S(1)}, f32[16,16,1]{2,1,0:T(8,128)S(1)}, u32[]{:S(2)}, u32[]{:S(2)}) collective-permute-start(f32[16,16,1]{2,1,0:T(8,128)S(1)} %get-tuple-element.44), channel_id=1, source_target_pairs={{64,0},{128,64},{192,128},{65,1},{129,65},{193,129},{66,2},{130,66... | collective-permute-start | bytes 3080 | tf_op jit(solution)/shard_map/ppermute | solution.py:23
  276.4 6.8 collective-permute-start.16
  284.5 6.2 collective-permute-start.18
  288.1 6.7 collective-permute-start.19
  301.9 7.5 %collective-permute-start.22 = (f32[18,1,130]{2,1,0:T(1,128)S(1)}, f32[18,1,130]{2,1,0:T(1,128)S(1)}, u32[]{:S(2)}, u32[]{:S(2)}) collective-permute-start(f32[18,1,130]{2,1,0:T(1,128)S(1)} %get-tuple-element.10), channel_id=1, source_target_pairs={{1,0},{2,1},{3,2},{4,3},{5,4},{6,5},{7,6},{9,8},{10,9},{11,10},{12... | collective-permute-start | bytes 28088 | tf_op jit(solution)/shard_map/ppermute | solution.py:23
  318.4 6.8 collective-permute-start.26
  319.7 6.3 collective-permute-start.27
  326.2 8.6 %collective-permute-start.28 = (f32[18,1,130]{2,1,0:T(1,128)S(1)}, f32[18,1,130]{2,1,0:T(1,128)S(1)}, u32[]{:S(2)}, u32[]{:S(2)}) collective-permute-start(f32[18,1,130]{2,1,0:T(1,128)S(1)} %get-tuple-element.8), channel_id=1, source_target_pairs={{1,0},{2,1},{3,2},{4,3},{5,4},{6,5},{7,6},{9,8},{10,9},{11,10},{12... | collective-permute-start | bytes 28088 | tf_op jit(solution)/shard_map/ppermute | solution.py:23
  328.4 7.4 %collective-permute-start.29 = (f32[18,1,130]{2,1,0:T(1,128)S(1)}, f32[18,1,130]{2,1,0:T(1,128)S(1)}, u32[]{:S(2)}, u32[]{:S(2)}) collective-permute-start(f32[18,1,130]{2,1,0:T(1,128)S(1)} %get-tuple-element.9), channel_id=1, source_target_pairs={{0,1},{1,2},{2,3},{3,4},{4,5},{5,6},{6,7},{8,9},{9,10},{10,11},{11... | collective-permute-start | bytes 28088 | tf_op jit(solution)/shard_map/ppermute | solution.py:21
  343.6 7.1 %collective-permute-start.32 = (f32[1,16,130]{2,1,0:T(8,128)S(1)}, f32[1,16,130]{2,1,0:T(8,128)S(1)}, u32[]{:S(2)}, u32[]{:S(2)}) collective-permute-start(f32[1,16,130]{2,1,0:T(8,128)S(1)} %get-tuple-element.23), channel_id=1, source_target_pairs={{8,0},{16,8},{24,16},{32,24},{40,32},{48,40},{56,48},{9,1},{17,9},... | collective-permute-start | bytes 24968 | tf_op jit(solution)/shard_map/ppermute | solution.py:23
  344.9 6.6 collective-permute-start.33
  351.7 8.4 %collective-permute-start.34 = (f32[18,1,130]{2,1,0:T(1,128)S(1)}, f32[18,1,130]{2,1,0:T(1,128)S(1)}, u32[]{:S(2)}, u32[]{:S(2)}) collective-permute-start(f32[18,1,130]{2,1,0:T(1,128)S(1)} %get-tuple-element.6), channel_id=1, source_target_pairs={{1,0},{2,1},{3,2},{4,3},{5,4},{6,5},{7,6},{9,8},{10,9},{11,10},{12... | collective-permute-start | bytes 28088 | tf_op jit(solution)/shard_map/ppermute | solution.py:23
  353.6 7.4 %collective-permute-start.35 = (f32[18,1,130]{2,1,0:T(1,128)S(1)}, f32[18,1,130]{2,1,0:T(1,128)S(1)}, u32[]{:S(2)}, u32[]{:S(2)}) collective-permute-start(f32[18,1,130]{2,1,0:T(1,128)S(1)} %get-tuple-element.7), channel_id=1, source_target_pairs={{0,1},{1,2},{2,3},{3,4},{4,5},{5,6},{6,7},{8,9},{9,10},{10,11},{11... | collective-permute-start | bytes 28088 | tf_op jit(solution)/shard_map/ppermute | solution.py:21
  368.9 7.1 %collective-permute-start.38 = (f32[1,16,130]{2,1,0:T(8,128)S(1)}, f32[1,16,130]{2,1,0:T(8,128)S(1)}, u32[]{:S(2)}, u32[]{:S(2)}) collective-permute-start(f32[1,16,130]{2,1,0:T(8,128)S(1)} %get-tuple-element.21), channel_id=1, source_target_pairs={{8,0},{16,8},{24,16},{32,24},{40,32},{48,40},{56,48},{9,1},{17,9},... | collective-permute-start | bytes 24968 | tf_op jit(solution)/shard_map/ppermute | solution.py:23
  370.2 6.6 collective-permute-start.39
  377.0 8.4 %collective-permute-start.40 = (f32[18,1,130]{2,1,0:T(1,128)S(1)}, f32[18,1,130]{2,1,0:T(1,128)S(1)}, u32[]{:S(2)}, u32[]{:S(2)}) collective-permute-start(f32[18,1,130]{2,1,0:T(1,128)S(1)} %get-tuple-element.4), channel_id=1, source_target_pairs={{1,0},{2,1},{3,2},{4,3},{5,4},{6,5},{7,6},{9,8},{10,9},{11,10},{12... | collective-permute-start | bytes 28088 | tf_op jit(solution)/shard_map/ppermute | solution.py:23
  378.9 7.4 %collective-permute-start.41 = (f32[18,1,130]{2,1,0:T(1,128)S(1)}, f32[18,1,130]{2,1,0:T(1,128)S(1)}, u32[]{:S(2)}, u32[]{:S(2)}) collective-permute-start(f32[18,1,130]{2,1,0:T(1,128)S(1)} %get-tuple-element.5), channel_id=1, source_target_pairs={{0,1},{1,2},{2,3},{3,4},{4,5},{5,6},{6,7},{8,9},{9,10},{10,11},{11... | collective-permute-start | bytes 28088 | tf_op jit(solution)/shard_map/ppermute | solution.py:21
  394.2 7.1 %collective-permute-start.44 = (f32[1,16,130]{2,1,0:T(8,128)S(1)}, f32[1,16,130]{2,1,0:T(8,128)S(1)}, u32[]{:S(2)}, u32[]{:S(2)}) collective-permute-start(f32[1,16,130]{2,1,0:T(8,128)S(1)} %get-tuple-element.19), channel_id=1, source_target_pairs={{8,0},{16,8},{24,16},{32,24},{40,32},{48,40},{56,48},{9,1},{17,9},... | collective-permute-start | bytes 24968 | tf_op jit(solution)/shard_map/ppermute | solution.py:23
  395.5 6.6 collective-permute-start.45
  402.2 16.1 %collective-permute-start.46 = (f32[18,1,130]{2,1,0:T(1,128)S(1)}, f32[18,1,130]{2,1,0:T(1,128)S(1)}, u32[]{:S(2)}, u32[]{:S(2)}) collective-permute-start(f32[18,1,130]{2,1,0:T(1,128)S(1)} %get-tuple-element.2), channel_id=1, source_target_pairs={{1,0},{2,1},{3,2},{4,3},{5,4},{6,5},{7,6},{9,8},{10,9},{11,10},{12... | collective-permute-start | bytes 28088 | tf_op jit(solution)/shard_map/ppermute | solution.py:23
  404.2 14.2 %collective-permute-start.47 = (f32[18,1,130]{2,1,0:T(1,128)S(1)}, f32[18,1,130]{2,1,0:T(1,128)S(1)}, u32[]{:S(2)}, u32[]{:S(2)}) collective-permute-start(f32[18,1,130]{2,1,0:T(1,128)S(1)} %get-tuple-element.3), channel_id=1, source_target_pairs={{0,1},{1,2},{2,3},{3,4},{4,5},{5,6},{6,7},{8,9},{9,10},{10,11},{11... | collective-permute-start | bytes 28088 | tf_op jit(solution)/shard_map/ppermute | solution.py:21
  (31 other events, 913.5 us)
where the time goes:
time: 715 us; the launch traced here: 706 us
  blocking collectives  257 us (36%)
  waiting for transfers between devices  177 us (25%)
  starting transfers between devices  168 us (23%)
  local copies, waits for them, and re-layouts  72.7 us (10%)
  matrix products  18.2 us (3%)
  other arithmetic  11.1 us (2%)
    unnamed x1, blocking collectives  250 us
    ppermute x24, waiting for transfers between devices, extended(): lax.ppermute(head, axis, [((i + 1) % count, i) for i in range(ends)])  109 us
    ppermute x24, starting transfers between devices, extended(): lax.ppermute(tail, axis, [(i, (i + 1) % count) for i in range(ends)])  95.5 us
    all_to_all x1, waiting for transfers between devices, local(): lax.all_to_all(buffer, 'fluid', split_axis=0, concat_axis=0, tiled=True)  45.2 us
    ppermute x24, starting transfers between devices, extended(): lax.ppermute(head, axis, [((i + 1) % count, i) for i in range(ends)])  42.8 us
    concatenate x1, local copies, waits for them, and re-layouts, local(): jnp.concatenate([previous_thermal_states.reshape(previous_thermal_states....  19.5 us
    ppermute x24, waiting for transfers between devices, extended(): lax.ppermute(tail, axis, [(i, (i + 1) % count) for i in range(ends)])  18.8 us
    scatter x1, local copies, waits for them, and re-layouts, local(): labels_out = jnp.full((count_all * capacity,), -1.0, jnp.float32).at[slot...  15.5 us
  transfers between devices with their start and end apart: 52, of which 32 were waited for; matrix products, arithmetic and copies ran while one was open for 6% of the time, Pallas kernels for 0%

commit v1 on v0

v1 whole, which is shorter than its diff:
```python
import functools

import jax
import jax.numpy as jnp
from jax import lax
from jax.experimental import pallas as pl
from jax.experimental.pallas import tpu as pltpu
from jax.sharding import Mesh
from jax.sharding import PartitionSpec as P

STEPS = 8
HALO = 8
HIST = 56
SNAPS = HIST + STEPS
SLOTS = 32
LINES = 256
LANES = 128
QUADS = 4
PEERS = 64
PEER_ROWS = QUADS * SLOTS + 8
CHUNK = 256
TILE = 16
WIDE = TILE + 2 * HALO

rate_step = 0.16
source_gain = 0.1

SX = ("sxq", "sxp")
PLANE = ("fluid", "sxp", "sy")
ALL = ("fluid", "sxq", "sxp", "sy")

f32 = jnp.float32
bf16 = jnp.bfloat16


def dot_nt(a, b, precision=None):
    return lax.dot_general(
        a, b, (((1,), (1,)), ((), ())), precision=precision, preferred_element_type=f32
    )


def split(x):
    high = x.astype(bf16)
    return high, (x - high.astype(f32)).astype(bf16)


def rank_kernel(shift_ref, owner_ref, line_ref, slot_ref, label_ref, carry_ref):
    carry_ref[...] = jnp.zeros_like(carry_ref)
    label_ref[...] = jnp.zeros_like(label_ref)
    rows = lax.broadcasted_iota(jnp.int32, (CHUNK, CHUNK), 0)
    cols = lax.broadcasted_iota(jnp.int32, (CHUNK, CHUNK), 1)
    earlier = jnp.where(rows < cols, 1.0, 0.0).astype(bf16)
    places = lax.broadcasted_iota(jnp.int32, (LANES, CHUNK), 0)
    shift = shift_ref[0]

    def body(c, _):
        owner = owner_ref[pl.ds(c, 1), :]
        fluid, sx, sy = owner >> 6, (owner >> 3) & 7, owner & 7
        peer = (fluid * 2 + (sx & 1)) * 8 + sy
        quad = sx >> 1
        match = rows == peer * QUADS + quad
        hit = jnp.where(match, 1.0, 0.0)
        hit16 = hit.astype(bf16)
        before = jnp.dot(hit16, earlier, preferred_element_type=f32)
        rank = jnp.sum(jnp.where(match, before + carry_ref[...], 0.0), axis=0, keepdims=True)
        carry_ref[...] += before[:, CHUNK - 1 :] + hit[:, CHUNK - 1 :]
        rank = rank.astype(jnp.int32)
        slot_ref[pl.ds(c, 1), :] = peer * PEER_ROWS + quad * SLOTS + rank
        value = (line_ref[pl.ds(c, 1), :] + 1).astype(f32)
        spread = jnp.where(places == rank + shift, value, 0.0).astype(bf16)
        label_ref[...] += dot_nt(hit16, spread)
        return 0

    lax.fori_loop(0, owner_ref.shape[0], body, 0)


def pack_kernel(slot_ref, blocks_ref, label_ref, out_ref):
    def clear(i, _):
        out_ref[pl.ds(pl.multiple_of(i * PEER_ROWS, 8), PEER_ROWS), :] = jnp.zeros(
            (PEER_ROWS, LANES), f32
        )
        return 0

    lax.fori_loop(0, PEERS, clear, 0)
    for h in range(PEERS // 2):
        for e in range(2):
            at = (2 * h + e) * PEER_ROWS + QUADS * SLOTS
            out_ref[at : at + QUADS, :] = label_ref[8 * h + 4 * e : 8 * h + 4 * e + 4, :]

    step = 32
    per_row = slot_ref.shape[1] // step

    def place(i, _):
        row, col = i // per_row, (i % per_row) * step
        for t in range(step):
            slot = slot_ref[row, col + t]
            out_ref[pl.ds(slot, 1), :] = blocks_ref[pl.ds(i * step + t, 1), :]
        return 0

    lax.fori_loop(0, blocks_ref.shape[0] // step, place, 0)


def deposit_kernel(quad_ref, block_ref, map_ref, *rest):
    outs, total = rest[:QUADS], rest[QUADS]
    g = pl.program_id(0)

    @pl.when(g == 0)
    def _():
        total[...] = jnp.zeros_like(total)

    lines = lax.broadcasted_iota(jnp.int32, (LINES, LANES), 0).astype(f32) + 1.0
    for q in range(QUADS):
        marks = []
        for half in range(2):
            at = QUADS * SLOTS + q
            label = block_ref[4 * half, at : at + 1, :]
            for t in range(1, 4):
                label = label + block_ref[4 * half + t, at : at + 1, :]
            marks.append(jnp.where(lines == label, 1.0, 0.0).astype(bf16))
        mark = jnp.concatenate(marks, axis=1)
        values = block_ref[:, q * SLOTS : (q + 1) * SLOTS, :].reshape(8 * SLOTS, LANES)
        high, low = split(values)
        total[q] += jnp.dot(
            mark, jnp.concatenate([high, low], axis=1), preferred_element_type=f32
        )

    @pl.when(g == pl.num_programs(0) - 1)
    def _():
        for k in range(QUADS):
            both = total[(quad_ref[0] + k) % QUADS]
            outs[k][...] = source_gain * jnp.dot(
                both[:, :LANES] + both[:, LANES:],
                map_ref[...],
                precision=lax.Precision.HIGHEST,
                preferred_element_type=f32,
            )


def step_kernel(
    start_ref,
    source_ref,
    source_up,
    source_down,
    source_left,
    source_right,
    past_gram,
    history,
    field_ref,
    rows_ref,
    now_m,
    now_e,
    next_m,
    next_e,
    src_m,
    src_e,
    snaps,
    past,
    acc,
    sem,
):
    load = pltpu.make_async_copy(history, past, sem)
    load.start()
    pad = WIDE
    count = WIDE * WIDE
    for k, (now, src) in enumerate(((now_m, src_m), (now_e, src_e))):
        now[0:pad, :] = jnp.zeros((pad, LANES), f32)
        now[pad + count :, :] = jnp.zeros((pad, LANES), f32)
        now[pad : pad + count, :] = start_ref[2 * k]
        for x in range(WIDE):
            src[x * WIDE : x * WIDE + HALO, :] = source_left[k, x]
            src[x * WIDE + WIDE - HALO : (x + 1) * WIDE, :] = source_right[k, x]
            if x < HALO:
                middle = source_up[k, x]
            elif x < HALO + TILE:
                middle = source_ref[k, x - HALO]
            else:
                middle = source_down[k, x - HALO - TILE]
            src[x * WIDE + HALO : x * WIDE + HALO + TILE, :] = middle
    lane = lax.broadcasted_iota(jnp.int32, (WIDE, LANES), 1)
    first, last = lane == 0, lane == LANES - 1

    def advance(a_m, a_e, b_m, b_e, s):
        def body(x, _):
            r = pl.multiple_of(x * WIDE, 8)
            at = lambda off: pl.ds(r + pad + off, WIDE)
            own = pl.ds(r, WIDE)
            m, e = a_m[at(0), :], a_e[at(0), :]
            roll = lambda v, d: pltpu.roll(v, d % LANES, 1)
            mr, er, ml, el = roll(m, 1), roll(e, 1), roll(m, -1), roll(e, -1)
            sides = (
                (a_m, b_m, m, jnp.where(first, er, mr) + jnp.where(last, el, ml), 1, src_m),
                (a_e, b_e, e, jnp.where(first, mr, er) + jnp.where(last, ml, el), 3, src_e),
            )
            for a, b, v, beside, d, src in sides:
                beside = beside + (a[at(-WIDE), :] + a[at(WIDE), :])
                beside = beside + (a[at(-1), :] + a[at(1), :])
                b[at(0), :] = v + start_ref[d, own, :] * (beside - 6.0 * v) + src[own, :]
            return 0

        lax.fori_loop(s + 1, WIDE - 1 - s, body, 0)
        for x in range(TILE):
            r = pad + (x + HALO) * WIDE + HALO
            for h in range(2):
                snaps[x * 2 + h, 8 * s : 8 * s + 8, :] = b_m[r + 8 * h : r + 8 * h + 8, :]

    for s in range(0, STEPS, 2):
        if s == 0:
            next_m[...] = jnp.zeros_like(next_m)
            next_e[...] = jnp.zeros_like(next_e)
        advance(now_m, now_e, next_m, next_e, s)
        advance(next_m, next_e, now_m, now_e, s + 1)
    for x in range(TILE):
        for h in range(2):
            field_ref[x, 8 * h : 8 * h + 8, :] = snaps[x * 2 + h, 8 * (STEPS - 1) :, :]

    load.wait()
    acc[...] = jnp.zeros_like(acc)
    tall = 8 * HIST

    def gram(i, _):
        x, h = (i // 2) * 2, i % 2
        new = [snaps[(x + e) * 2 + h] for e in range(2)]
        old = [
            past[:, x + e, pl.ds(pl.multiple_of(h * 8, 8), 8), :].reshape(tall, LANES)
            for e in range(2)
        ]
        new_high, new_low = split(jnp.concatenate(new, axis=1))
        old_high, old_low = split(jnp.concatenate(old, axis=1))
        right = jnp.concatenate([new_high, new_low], axis=0)
        acc[0:tall, :] += dot_nt(old_high, right) + dot_nt(old_low, right)
        acc[tall:, :] += dot_nt(new_high, right) + dot_nt(new_low, right)
        return 0

    lax.fori_loop(0, TILE, gram, 0)
    y = lax.broadcasted_iota(jnp.int32, acc.shape, 0) % 8
    y_new = lax.broadcasted_iota(jnp.int32, acc.shape, 1) % 8
    products = jnp.where(y == y_new, acc[...], 0.0).reshape(SNAPS, 8, 2 * 8 * STEPS).sum(axis=1)
    snap_of = lambda shape, dim: (lax.broadcasted_iota(jnp.int32, shape, dim) % 64) // 8
    wide, tallest = (2 * 8 * STEPS, SNAPS), (STEPS, 2 * 8 * STEPS)
    pick = snap_of(wide, 0) == lax.broadcasted_iota(jnp.int32, wide, 1) - HIST
    right = jnp.dot(
        products,
        jnp.where(pick, 1.0, 0.0),
        precision=lax.Precision.HIGHEST,
        preferred_element_type=f32,
    )
    pick = snap_of(tallest, 1) == lax.broadcasted_iota(jnp.int32, tallest, 0)
    low = dot_nt(jnp.where(pick, 1.0, 0.0), products, lax.Precision.HIGHEST)
    upper = past_gram[...] + right[:HIST]
    for f in range(rows_ref.shape[0] // SNAPS):
        rows_ref[f * SNAPS : f * SNAPS + HIST, :] = upper
        rows_ref[f * SNAPS + HIST : (f + 1) * SNAPS, :] = low


def up_chain(axis):
    count = lax.axis_size(axis)
    return [(i, i + 1) for i in range(count - 1)]


def down_chain(axis):
    count = lax.axis_size(axis)
    return [(i + 1, i) for i in range(count - 1)]


def beyond(cells):
    after = lax.ppermute(cells, "fluid", down_chain("fluid"))
    before = lax.ppermute(cells, "fluid", up_chain("fluid"))
    lane = lax.broadcasted_iota(jnp.int32, cells.shape, cells.ndim - 1)
    return jnp.where(lane < LANES // 2, after, before)


def slabs(cells):
    up = lax.ppermute(cells[:, TILE - HALO :], SX, up_chain(SX))
    down = lax.ppermute(cells[:, :HALO], SX, down_chain(SX))
    tall = jnp.concatenate([up, cells, down], axis=1)
    left = lax.ppermute(tall[:, :, TILE - HALO :], "sy", up_chain("sy"))
    right = lax.ppermute(tall[:, :, :HALO], "sy", down_chain("sy"))
    return up, down, tall, left, right


def whole(shape):
    return pl.BlockSpec(shape, lambda *_: (0,) * len(shape))


def local(
    opening_conductor_warmth,
    cellwise_diffusivity,
    previous_thermal_states,
    boundary_heat_rate_pieces,
    receiving_processor_per_piece,
    boundary_line_position_in_tile,
    piece_to_solid_line_mapping,
):
    blocks = boundary_heat_rate_pieces.shape[0]
    chunks = blocks // CHUNK
    vmem = pl.BlockSpec(memory_space=pltpu.VMEM)
    smem = pl.BlockSpec(memory_space=pltpu.SMEM)
    limit = pltpu.CompilerParams(vmem_limit_bytes=48 * 1024 * 1024)

    with jax.named_scope("rank"):
        shift = (lax.axis_index("sy") % 4 * SLOTS).astype(jnp.int32).reshape(1)
        slots, labels = pl.pallas_call(
            rank_kernel,
            out_shape=(
                jax.ShapeDtypeStruct((chunks, CHUNK), jnp.int32),
                jax.ShapeDtypeStruct((CHUNK, LANES), f32),
            ),
            in_specs=[smem, vmem, vmem],
            out_specs=(vmem, vmem),
            scratch_shapes=[pltpu.VMEM((CHUNK, 1), f32)],
            compiler_params=limit,
        )(
            shift,
            receiving_processor_per_piece.reshape(chunks, CHUNK),
            boundary_line_position_in_tile.reshape(chunks, CHUNK),
        )

    with jax.named_scope("pack"):
        packed = pl.pallas_call(
            pack_kernel,
            out_shape=jax.ShapeDtypeStruct((PEERS * PEER_ROWS, LANES), f32),
            in_specs=[smem, vmem, vmem],
            out_specs=vmem,
            compiler_params=limit,
        )(slots, boundary_heat_rate_pieces, labels)

    with jax.named_scope("early_halo"):
        pair = jnp.stack([opening_conductor_warmth, rate_step * cellwise_diffusivity])
        pair = jnp.concatenate([pair, beyond(pair)])
        _, _, tall, left, right = slabs(pair)
        start = jnp.concatenate([left, tall, right], axis=2).reshape(4, WIDE * WIDE, LANES)
        packed, start = lax.optimization_barrier((packed, start))

    with jax.named_scope("exchange"):
        received = lax.all_to_all(
            packed.reshape(PEERS, PEER_ROWS, LANES), PLANE, split_axis=0, concat_axis=0, tiled=True
        )

    with jax.named_scope("history"):
        flat = previous_thermal_states.reshape(HIST, -1)
        cells = float(flat.shape[1] * lax.axis_size(ALL))
        past_gram = jnp.dot(
            flat, flat.T, precision=lax.Precision.HIGHEST, preferred_element_type=f32
        )
        past_gram = jnp.pad(past_gram, ((0, 0), (0, STEPS)))

    with jax.named_scope("deposit"):
        part = jax.ShapeDtypeStruct((LINES, LANES), f32)
        parts = pl.pallas_call(
            deposit_kernel,
            out_shape=(part,) * QUADS,
            grid_spec=pltpu.PrefetchScalarGridSpec(
                num_scalar_prefetch=1,
                grid=(PEERS // 8,),
                in_specs=[
                    pl.BlockSpec((8, PEER_ROWS, LANES), lambda g, _: (g, 0, 0)),
                    whole((LANES, LANES)),
                ],
                out_specs=(whole((LINES, LANES)),) * QUADS,
                scratch_shapes=[pltpu.VMEM((QUADS, LINES, 2 * LANES), f32)],
            ),
            compiler_params=limit,
        )(lax.axis_index("sxq").astype(jnp.int32).reshape(1), received, piece_to_solid_line_mapping)
        source = parts[0]
        for k in range(1, QUADS):
            ring = [(i, (i + k) % QUADS) for i in range(QUADS)]
            source = source + lax.ppermute(parts[k], "sxq", ring)
        source = source.reshape(1, TILE, TILE, LANES)

    with jax.named_scope("source_halo"):
        source = jnp.concatenate([source, beyond(source)])
        up, down, _, left, right = slabs(source)

    with jax.named_scope("steps"):
        rows = lax.axis_size("fluid") * SNAPS
        grid_rows = WIDE * WIDE
        buffer = pltpu.VMEM((grid_rows + 2 * WIDE, LANES), f32)
        field, gram_rows = pl.pallas_call(
            step_kernel,
            out_shape=(
                jax.ShapeDtypeStruct((TILE, TILE, LANES), f32),
                jax.ShapeDtypeStruct((rows, SNAPS), f32),
            ),
            in_specs=[vmem] * 7 + [pl.BlockSpec(memory_space=pl.ANY)],
            out_specs=(vmem, vmem),
            scratch_shapes=[
                buffer,
                buffer,
                buffer,
                buffer,
                pltpu.VMEM((grid_rows, LANES), f32),
                pltpu.VMEM((grid_rows, LANES), f32),
                pltpu.VMEM((TILE * 2, 8 * STEPS, LANES), f32),
                pltpu.VMEM((HIST, TILE, TILE, LANES), f32),
                pltpu.VMEM((8 * SNAPS, 2 * 8 * STEPS), f32),
                pltpu.SemaphoreType.DMA,
            ],
            compiler_params=limit,
        )(start, source, up, down, left, right, past_gram, previous_thermal_states)

    with jax.named_scope("gram_sum"):
        shares = lax.all_to_all(gram_rows, ALL, split_axis=0, concat_axis=0, tiled=True)
        inner_product_matrix = jnp.sum(shares, axis=0, keepdims=True) / cells
    return field, inner_product_matrix


def solution(mesh):
    fluid, sx, sy = (mesh.shape[name] for name in ("fluid", "sx", "sy"))
    inner = Mesh(mesh.devices.reshape(fluid, sx // 2, 2, sy), ALL)
    cell = P(SX, "sy", "fluid")
    wall = P(ALL, None)
    return jax.shard_map(
        local,
        mesh=inner,
        in_specs=(cell, cell, P(None, SX, "sy", "fluid"), wall, wall, wall, P()),
        out_specs=(cell, P((*SX, "sy"), None)),
        check_vma=False,
    )
```

time: 715 us -> 243 us (0.34); the launches traced: 706 us -> 242 us
  blocking collectives: 257 us -> 25 us
  starting transfers between devices: 168 us -> 57.9 us
  waiting for transfers between devices: 177 us -> 79.1 us
  local copies, waits for them, and re-layouts: 72.7 us -> 1.74 us
  Pallas kernels: 0 us -> 51.2 us
    unnamed x1 -> x0, blocking collectives: 250 us -> none
    ppermute x48 -> x15, waiting for transfers between devices: 128 us -> 22.5 us  [the longest x3 8.38 us: local(): source = source + lax.ppermute(parts[k], 'sxq', ring)]
    ppermute x48 -> x15, starting transfers between devices: 138 us -> 47.3 us  [the longest x2 9.74 us: slabs(): up = lax.ppermute(cells[:, TILE - HALO:], SX, up_chain(SX))]
    pallas_call x0 -> x4, Pallas kernels: none -> 51.2 us  [the longest x1 22.9 us: local(): pl.pallas_call(step_kernel, out_shape=(jax.ShapeDtypeStruct((TILE, TILE,...]
    scatter x2 -> x0, local copies, waits for them, and re-layouts: 28.7 us -> none  [the longest x1 15.5 us: local(): labels_out = jnp.full((count_all * capacity,), -1.0, jnp.float32).at[slot...]
    all_to_all x0 -> x1, blocking collectives: none -> 25 us  [local(): lax.all_to_all(gram_rows, ALL, split_axis=0, concat_axis=0, tiled=True)]
    concatenate x1 -> x0, local copies, waits for them, and re-layouts: 19.5 us -> none  [local(): jnp.concatenate([previous_thermal_states.reshape(previous_thermal_states....]
    all_to_all x4 -> x1, starting transfers between devices: 30 us -> 10.7 us  [local(): lax.all_to_all(packed.reshape(PEERS, PEER_ROWS, LANES), PLANE, split_axis...]
  transfers between devices with their start and end apart: 52 -> 16, of which waited for: 32 -> 10; matrix products, arithmetic and copies ran while one was open for 6% -> 9% of each run, Pallas kernels for 0% -> 9%
where the time goes in v1:
time: 243 us; the launch traced here: 242 us
  waiting for transfers between devices  79.1 us (33%)
  starting transfers between devices  57.9 us (24%)
  Pallas kernels  51.2 us (21%)
  blocking collectives  25 us (10%)
  matrix products  19.5 us (8%)
  other arithmetic  6.63 us (3%)
    all_to_all x1, waiting for transfers between devices, local(): lax.all_to_all(packed.reshape(PEERS, PEER_ROWS, LANES), PLANE, split_axis...  56.6 us
    all_to_all x1, blocking collectives, local(): lax.all_to_all(gram_rows, ALL, split_axis=0, concat_axis=0, tiled=True)  25 us
    pallas_call x1, Pallas kernels, local(): pl.pallas_call(step_kernel, out_shape=(jax.ShapeDtypeStruct((TILE, TILE,...  22.9 us
    dot_general x1, matrix products, local(): jnp.dot(flat, flat.T, precision=lax.Precision.HIGHEST, preferred_element_...  19.5 us
    pallas_call x1, Pallas kernels, local(): pl.pallas_call(pack_kernel, out_shape=jax.ShapeDtypeStruct((PEERS * PEER_...  14.4 us
    all_to_all x1, starting transfers between devices, local(): lax.all_to_all(packed.reshape(PEERS, PEER_ROWS, LANES), PLANE, split_axis...  10.7 us
    ppermute x2, starting transfers between devices, slabs(): up = lax.ppermute(cells[:, TILE - HALO:], SX, up_chain(SX))  9.74 us
    ppermute x3, starting transfers between devices, local(): source = source + lax.ppermute(parts[k], 'sxq', ring)  9.21 us
  transfers between devices with their start and end apart: 16, of which 10 were waited for; matrix products, arithmetic and copies ran while one was open for 9% of the time, Pallas kernels for 9%

profile of v1, /device:TPU:1, one launch (start us, length us, event | category | flops | bytes accessed | tf_op | source)
XLA Modules:
  0.0 242.1 jit_solution(13548544492702815525)
XLA Ops:
  2.5 1.3 collective-permute-start
  3.8 4.7 %collective-permute-start.1 = (f32[2,16,16,128]{3,2,1,0:T(8,128)S(1)}, f32[2,16,16,128]{3,2,1,0:T(8,128)S(1)}, u32[]{:S(2)}, u32[]{:S(2)}) collective-permute-start(f32[2,16,16,128]{3,2,1,0:T(8,128)S(1)} %pad_maximum_fusion.5), channel_id=1, source_target_pairs={{0,64},{64,128},{128,192},{1,65},{65,129},{129,193},{2,66},{66,130... | collective-permute-start | bytes 786440 | tf_op jit(solution)/shard_map/early_halo/ppermute | solution.py:267
  8.5 1.8 collective-permute-done
  10.3 1.5 collective-permute-done.1
  12.8 1.3 collective-permute-start.3
  14.2 5.8 %collective-permute-start.2 = (f32[4,8,16,128]{3,2,1,0:T(8,128)S(1)}, f32[4,8,16,128]{3,2,1,0:T(8,128)S(1)}, u32[]{:S(2)}, u32[]{:S(2)}) collective-permute-start(f32[4,8,16,128]{3,2,1,0:T(8,128)S(1)} %get-tuple-element.26), channel_id=1, source_target_pairs={{0,8},{8,16},{16,24},{24,32},{32,40},{40,48},{48,56},{1,9},{9,17},... | collective-permute-start | bytes 786440 | tf_op jit(solution)/shard_map/early_halo/ppermute | solution.py:273
  20.0 2.2 collective-permute-done.3
  22.2 1.1 collective-permute-done.2
  23.3 1.1 fusion.7
  24.4 5.1 %collective-permute-start.5 = (f32[4,32,8,128]{3,2,1,0:T(8,128)}, f32[4,32,8,128]{3,2,1,0:T(8,128)}, u32[]{:S(2)}, u32[]{:S(2)}) collective-permute-start(f32[4,32,8,128]{3,2,1,0:T(8,128)} %get-tuple-element.23), channel_id=1, source_target_pairs={{1,0},{2,1},{3,2},{4,3},{5,4},{6,5},{7,6},{9,8},{10,9},{11,10},{12... | collective-permute-start | bytes 1572872 | tf_op jit(solution)/shard_map/early_halo/ppermute | solution.py:277
  29.5 3.0 %collective-permute-start.4 = (f32[4,32,8,128]{3,2,1,0:T(8,128)}, f32[4,32,8,128]{3,2,1,0:T(8,128)}, u32[]{:S(2)}, u32[]{:S(2)}) collective-permute-start(f32[4,32,8,128]{3,2,1,0:T(8,128)} %get-tuple-element.22), channel_id=1, source_target_pairs={{0,1},{1,2},{2,3},{3,4},{4,5},{5,6},{6,7},{8,9},{9,10},{10,11},{11... | collective-permute-start | bytes 1572872 | tf_op jit(solution)/shard_map/early_halo/ppermute | solution.py:276
  34.5 7.1 %rank.1 = (s32[16,256]{1,0:T(8,128)S(1)}, f32[256,128]{1,0:T(8,128)S(1)}) custom-call(s32[1]{0:T(128)} %bitcast.shift_ref, s32[16,256]{1,0:T(8,128)S(1)} %reshape.39.owner_ref, s32[16,256]{1,0:T(8,128)S(1)} %reshape.40.line_ref), custom_call_target="tpu_custom_call" | custom-call | tf_op jit(solution)/shard_map/rank/pallas_call | solution.py:302
  41.7 14.4 %pack.1 = f32[8704,128]{1,0:T(8,128)} custom-call(s32[16,256]{1,0:T(8,128)S(1)} %get-tuple-element.12.slot_ref, f32[4096,128]{1,0:T(8,128)S(1)} %copy-done, f32[256,128]{1,0:T(8,128)S(1)} %get-tuple-element.13.label_ref), custom_call_target="tpu_custom_call" | custom-call | tf_op jit(solution)/shard_map/pack/pallas_call | solution.py:319
  56.1 1.4 pad_maximum_fusion
  57.5 10.7 %all-to-all-start = ((f32[64,136,128]{2,1,0:T(8,128)}), f32[64,136,128]{2,1,0:T(8,128)}, u32[]{:S(2)}, u32[]{:S(2)}) async-start(f32[64,136,128]{2,1,0:T(8,128)} %bitcast.21), calls=%async_computation | async-start | bytes 8912896 | tf_op jit(solution)/shard_map/exchange/all_to_all | solution.py:335
  68.2 56.6 %all-to-all-done.block_ref = f32[64,136,128]{2,1,0:T(8,128)} async-done(((f32[64,136,128]{2,1,0:T(8,128)}), f32[64,136,128]{2,1,0:T(8,128)}, u32[]{:S(2)}, u32[]{:S(2)}) %all-to-all-start) | async-done | bytes 4456480 | tf_op jit(solution)/shard_map/exchange/all_to_all | solution.py:335
  124.8 6.7 %deposit.1 = (f32[256,128]{1,0:T(8,128)S(1)}, f32[256,128]{1,0:T(8,128)S(1)}, f32[256,128]{1,0:T(8,128)S(1)}, f32[256,128]{1,0:T(8,128)S(1)}) custom-call(s32[1]{0:T(128)} %bitcast.4.quad_ref, f32[64,136,128]{2,1,0:T(8,128)} %all-to-all-done.block_ref, f32[128,128]{1,0:T(8,128)S(1)} %copy-done.1), custom_call_target="tpu_custom_call" | custom-call | tf_op jit(solution)/shard_map/deposit/pallas_call | solution.py:349
  131.5 5.9 %collective-permute-start.8 = (f32[256,128]{1,0:T(8,128)S(1)}, f32[256,128]{1,0:T(8,128)S(1)}, u32[]{:S(2)}, u32[]{:S(2)}) collective-permute-start(f32[256,128]{1,0:T(8,128)S(1)} %get-tuple-element.19), channel_id=1, source_target_pairs={{0,48},{16,0},{32,16},{48,32},{1,49},{17,1},{33,17},{49,33},{2,50}... | collective-permute-start | bytes 393224 | tf_op jit(solution)/shard_map/deposit/ppermute | solution.py:367
  138.5 2.2 collective-permute-start.6
  140.7 8.4 %collective-permute-done.7 = f32[256,128]{1,0:T(8,128)S(1)} collective-permute-done((f32[256,128]{1,0:T(8,128)S(1)}, f32[256,128]{1,0:T(8,128)S(1)}, u32[]{:S(2)}, u32[]{:S(2)}) %collective-permute-start.7) | collective-permute-done | bytes 131104 | tf_op jit(solution)/shard_map/deposit/ppermute | solution.py:367
  149.2 1.3 collective-permute-start.9
  150.5 4.0 %collective-permute-start.10 = (f32[1,16,16,128]{3,2,1,0:T(8,128)S(1)}, f32[1,16,16,128]{3,2,1,0:T(8,128)S(1)}, u32[]{:S(2)}, u32[]{:S(2)}) collective-permute-start(f32[1,16,16,128]{3,2,1,0:T(8,128)S(1)} %bitcast.27), channel_id=1, source_target_pairs={{0,64},{64,128},{128,192},{1,65},{65,129},{129,193},{2,66},{66,130... | collective-permute-start | bytes 393224 | tf_op jit(solution)/shard_map/source_halo/ppermute | solution.py:267
  154.5 1.4 collective-permute-done.9
  155.8 1.8 collective-permute-done.10
  157.7 3.9 %collective-permute-start.11 = (f32[2,8,16,128]{3,2,1,0:T(8,128)S(1)}, f32[2,8,16,128]{3,2,1,0:T(8,128)S(1)}, u32[]{:S(2)}, u32[]{:S(2)}) collective-permute-start(f32[2,8,16,128]{3,2,1,0:T(8,128)S(1)} %get-tuple-element.29), channel_id=1, source_target_pairs={{0,8},{8,16},{16,24},{24,32},{32,40},{40,48},{48,56},{1,9},{9,17},... | collective-permute-start | bytes 393224 | tf_op jit(solution)/shard_map/source_halo/ppermute | solution.py:273
  161.6 1.3 collective-permute-start.12
  163.5 3.8 %collective-permute-done.12.source_down = f32[2,8,16,128]{3,2,1,0:T(8,128)S(1)} collective-permute-done((f32[2,8,16,128]{3,2,1,0:T(8,128)S(1)}, f32[2,8,16,128]{3,2,1,0:T(8,128)S(1)}, u32[]{:S(2)}, u32[]{:S(2)}) %collective-permute-start.12) | collective-permute-done | bytes 131104 | tf_op jit(solution)/shard_map/source_halo/ppermute | solution.py:274
  167.4 3.8 %collective-permute-start.13 = (f32[2,32,8,128]{3,2,1,0:T(8,128)S(1)}, f32[2,32,8,128]{3,2,1,0:T(8,128)S(1)}, u32[]{:S(2)}, u32[]{:S(2)}) collective-permute-start(f32[2,32,8,128]{3,2,1,0:T(8,128)S(1)} %get-tuple-element.25), channel_id=1, source_target_pairs={{0,1},{1,2},{2,3},{3,4},{4,5},{5,6},{6,7},{8,9},{9,10},{10,11},{11... | collective-permute-start | bytes 786440 | tf_op jit(solution)/shard_map/source_halo/ppermute | solution.py:276
  171.2 2.6 %collective-permute-start.14 = (f32[2,32,8,128]{3,2,1,0:T(8,128)S(1)}, f32[2,32,8,128]{3,2,1,0:T(8,128)S(1)}, u32[]{:S(2)}, u32[]{:S(2)}) collective-permute-start(f32[2,32,8,128]{3,2,1,0:T(8,128)S(1)} %get-tuple-element.24), channel_id=1, source_target_pairs={{1,0},{2,1},{3,2},{4,3},{5,4},{6,5},{7,6},{9,8},{10,9},{11,10},{12... | collective-permute-start | bytes 786440 | tf_op jit(solution)/shard_map/source_halo/ppermute | solution.py:277
  173.8 19.5 %fusion.2 = f32[56,56]{1,0:T(8,128)S(1)} fusion(f32[56,16,16,128]{3,2,1,0:T(8,128)} %history.1), kind=kOutput, calls=%fused_computation.3 | convolution fusion | flops 1233125376 | bytes 7352576 | tf_op jit(solution)/shard_map/history/dot_general | solution.py:342
  193.4 22.9 %steps.1 = (f32[16,16,128]{2,1,0:T(8,128)}, f32[256,64]{1,0:T(8,128)S(1)}) custom-call(f32[4,1024,128]{2,1,0:T(8,128)S(1)} %bitcast.19, f32[2,16,16,128]{3,2,1,0:T(8,128)S(1)} %pad_maximum_fusion.4.source_ref, f32[2,8,16,128]{3,2,1,0:T(8,128)S(1)} %collective-permute-done.11.source_up, f32[2,8,16,128]{3,2,1,0:T(8,128)S(1)} %collective-permute-done.12.source_down, ...), custom_call_target="tpu_custom_call" | custom-call | tf_op jit(solution)/shard_map/steps/pallas_call | solution.py:378
  216.3 25.0 %all_to_all.14 = f32[256,1,64]{2,1,0:T(1,128)S(1)} all-to-all(f32[256,1,64]{2,1,0:T(1,128)S(1)} %bitcast.20), channel_id=1, replica_groups=mesh['fluid'=4,'sxq'=4,'sxp'=2,'sy'=8] {'fluid','sxq','sxp','sy'}, dimensions={0} | all-to-all | bytes 131072 | tf_op jit(solution)/shard_map/gram_sum/all_to_all | solution.py:402
  (39 shorter events, 7.6 us)
Async XLA Ops:
  0.6 22.6 %copy-start.2 = (f32[16,16,128]{2,1,0:T(8,128)S(1)}, f32[16,16,128]{2,1,0:T(8,128)}, u32[]{:S(2)}) copy-start(f32[16,16,128]{2,1,0:T(8,128)} %param.7) | copy-start | bytes 393220
  2.5 7.8 %collective-permute-start = (f32[2,16,16,128]{3,2,1,0:T(8,128)S(1)}, f32[2,16,16,128]{3,2,1,0:T(8,128)S(1)}, u32[]{:S(2)}, u32[]{:S(2)}) collective-permute-start(f32[2,16,16,128]{3,2,1,0:T(8,128)S(1)} %pad_maximum_fusion.5), channel_id=1, source_target_pairs={{64,0},{128,64},{192,128},{65,1},{129,65},{193,129},{66,2},{130,66... | collective-permute-start | bytes 786440 | tf_op jit(solution)/shard_map/early_halo/ppermute | solution.py:266
  3.8 8.0 %collective-permute-start.1 = (f32[2,16,16,128]{3,2,1,0:T(8,128)S(1)}, f32[2,16,16,128]{3,2,1,0:T(8,128)S(1)}, u32[]{:S(2)}, u32[]{:S(2)}) collective-permute-start(f32[2,16,16,128]{3,2,1,0:T(8,128)S(1)} %pad_maximum_fusion.5), channel_id=1, source_target_pairs={{0,64},{64,128},{128,192},{1,65},{65,129},{129,193},{2,66},{66,130... | collective-permute-start | bytes 786440 | tf_op jit(solution)/shard_map/early_halo/ppermute | solution.py:267
  12.8 9.3 %collective-permute-start.3 = (f32[4,8,16,128]{3,2,1,0:T(8,128)S(1)}, f32[4,8,16,128]{3,2,1,0:T(8,128)S(1)}, u32[]{:S(2)}, u32[]{:S(2)}) collective-permute-start(f32[4,8,16,128]{3,2,1,0:T(8,128)S(1)} %get-tuple-element.27), channel_id=1, source_target_pairs={{8,0},{16,8},{24,16},{32,24},{40,32},{48,40},{56,48},{9,1},{17,9},... | collective-permute-start | bytes 786440 | tf_op jit(solution)/shard_map/early_halo/ppermute | solution.py:274
  14.1 19.0 %copy-start.3 = (s32[4096,1]{0,1:T(1,128)S(1)}, s32[4096,1]{0,1:T(1,128)}, u32[]{:S(2)}) copy-start(s32[4096,1]{0,1:T(1,128)} %param.11) | copy-start | bytes 49156
  14.1 19.7 %copy-start.4 = (s32[4096,1]{0,1:T(1,128)S(1)}, s32[4096,1]{0,1:T(1,128)}, u32[]{:S(2)}) copy-start(s32[4096,1]{0,1:T(1,128)} %param.12) | copy-start | bytes 49156
  14.1 27.5 %copy-start = (f32[4096,128]{1,0:T(8,128)S(1)}, f32[4096,128]{1,0:T(8,128)}, u32[]{:S(2)}) copy-start(f32[4096,128]{1,0:T(8,128)} %blocks_ref.1) | copy-start | bytes 6291460
  14.2 9.1 %collective-permute-start.2 = (f32[4,8,16,128]{3,2,1,0:T(8,128)S(1)}, f32[4,8,16,128]{3,2,1,0:T(8,128)S(1)}, u32[]{:S(2)}, u32[]{:S(2)}) collective-permute-start(f32[4,8,16,128]{3,2,1,0:T(8,128)S(1)} %get-tuple-element.26), channel_id=1, source_target_pairs={{0,8},{8,16},{16,24},{24,32},{32,40},{40,48},{48,56},{1,9},{9,17},... | collective-permute-start | bytes 786440 | tf_op jit(solution)/shard_map/early_halo/ppermute | solution.py:273
  24.4 31.7 %collective-permute-start.5 = (f32[4,32,8,128]{3,2,1,0:T(8,128)}, f32[4,32,8,128]{3,2,1,0:T(8,128)}, u32[]{:S(2)}, u32[]{:S(2)}) collective-permute-start(f32[4,32,8,128]{3,2,1,0:T(8,128)} %get-tuple-element.23), channel_id=1, source_target_pairs={{1,0},{2,1},{3,2},{4,3},{5,4},{6,5},{7,6},{9,8},{10,9},{11,10},{12... | collective-permute-start | bytes 1572872 | tf_op jit(solution)/shard_map/early_halo/ppermute | solution.py:277
  29.5 26.6 %collective-permute-start.4 = (f32[4,32,8,128]{3,2,1,0:T(8,128)}, f32[4,32,8,128]{3,2,1,0:T(8,128)}, u32[]{:S(2)}, u32[]{:S(2)}) collective-permute-start(f32[4,32,8,128]{3,2,1,0:T(8,128)} %get-tuple-element.22), channel_id=1, source_target_pairs={{0,1},{1,2},{2,3},{3,4},{4,5},{5,6},{6,7},{8,9},{9,10},{10,11},{11... | collective-permute-start | bytes 1572872 | tf_op jit(solution)/shard_map/early_halo/ppermute | solution.py:276
  57.5 67.3 %copy-start.1 = (f32[128,128]{1,0:T(8,128)S(1)}, f32[128,128]{1,0:T(8,128)}, u32[]{:S(2)}) copy-start(f32[128,128]{1,0:T(8,128)} %map_ref.1) | copy-start | bytes 196612
  57.5 67.3 %all-to-all-start = ((f32[64,136,128]{2,1,0:T(8,128)}), f32[64,136,128]{2,1,0:T(8,128)}, u32[]{:S(2)}, u32[]{:S(2)}) async-start(f32[64,136,128]{2,1,0:T(8,128)} %bitcast.21), calls=%async_computation | async-start | bytes 8912896 | tf_op jit(solution)/shard_map/exchange/all_to_all | solution.py:335
  131.5 9.2 %collective-permute-start.8 = (f32[256,128]{1,0:T(8,128)S(1)}, f32[256,128]{1,0:T(8,128)S(1)}, u32[]{:S(2)}, u32[]{:S(2)}) collective-permute-start(f32[256,128]{1,0:T(8,128)S(1)} %get-tuple-element.19), channel_id=1, source_target_pairs={{0,48},{16,0},{32,16},{48,32},{1,49},{17,1},{33,17},{49,33},{2,50}... | collective-permute-start | bytes 393224 | tf_op jit(solution)/shard_map/deposit/ppermute | solution.py:367
  137.5 11.7 %collective-permute-start.7 = (f32[256,128]{1,0:T(8,128)S(1)}, f32[256,128]{1,0:T(8,128)S(1)}, u32[]{:S(2)}, u32[]{:S(2)}) collective-permute-start(f32[256,128]{1,0:T(8,128)S(1)} %get-tuple-element.18), channel_id=1, source_target_pairs={{0,32},{16,48},{32,0},{48,16},{1,33},{17,49},{33,1},{49,17},{2,34}... | collective-permute-start | bytes 393224 | tf_op jit(solution)/shard_map/deposit/ppermute | solution.py:367
  138.5 10.6 %collective-permute-start.6 = (f32[256,128]{1,0:T(8,128)S(1)}, f32[256,128]{1,0:T(8,128)S(1)}, u32[]{:S(2)}, u32[]{:S(2)}) collective-permute-start(f32[256,128]{1,0:T(8,128)S(1)} %get-tuple-element.17), channel_id=1, source_target_pairs={{0,16},{16,32},{32,48},{48,0},{1,17},{17,33},{33,49},{49,1},{2,18}... | collective-permute-start | bytes 393224 | tf_op jit(solution)/shard_map/deposit/ppermute | solution.py:367
  149.2 6.7 %collective-permute-start.9 = (f32[1,16,16,128]{3,2,1,0:T(8,128)S(1)}, f32[1,16,16,128]{3,2,1,0:T(8,128)S(1)}, u32[]{:S(2)}, u32[]{:S(2)}) collective-permute-start(f32[1,16,16,128]{3,2,1,0:T(8,128)S(1)} %bitcast.26), channel_id=1, source_target_pairs={{64,0},{128,64},{192,128},{65,1},{129,65},{193,129},{66,2},{130,66... | collective-permute-start | bytes 393224 | tf_op jit(solution)/shard_map/source_halo/ppermute | solution.py:266
  150.5 7.2 %collective-permute-start.10 = (f32[1,16,16,128]{3,2,1,0:T(8,128)S(1)}, f32[1,16,16,128]{3,2,1,0:T(8,128)S(1)}, u32[]{:S(2)}, u32[]{:S(2)}) collective-permute-start(f32[1,16,16,128]{3,2,1,0:T(8,128)S(1)} %bitcast.27), channel_id=1, source_target_pairs={{0,64},{64,128},{128,192},{1,65},{65,129},{129,193},{2,66},{66,130... | collective-permute-start | bytes 393224 | tf_op jit(solution)/shard_map/source_halo/ppermute | solution.py:267
  157.7 5.9 %collective-permute-start.11 = (f32[2,8,16,128]{3,2,1,0:T(8,128)S(1)}, f32[2,8,16,128]{3,2,1,0:T(8,128)S(1)}, u32[]{:S(2)}, u32[]{:S(2)}) collective-permute-start(f32[2,8,16,128]{3,2,1,0:T(8,128)S(1)} %get-tuple-element.29), channel_id=1, source_target_pairs={{0,8},{8,16},{16,24},{24,32},{32,40},{40,48},{48,56},{1,9},{9,17},... | collective-permute-start | bytes 393224 | tf_op jit(solution)/shard_map/source_halo/ppermute | solution.py:273
  161.6 5.7 %collective-permute-start.12 = (f32[2,8,16,128]{3,2,1,0:T(8,128)S(1)}, f32[2,8,16,128]{3,2,1,0:T(8,128)S(1)}, u32[]{:S(2)}, u32[]{:S(2)}) collective-permute-start(f32[2,8,16,128]{3,2,1,0:T(8,128)S(1)} %get-tuple-element.28), channel_id=1, source_target_pairs={{8,0},{16,8},{24,16},{32,24},{40,32},{48,40},{56,48},{9,1},{17,9},... | collective-permute-start | bytes 393224 | tf_op jit(solution)/shard_map/source_halo/ppermute | solution.py:274
  167.4 25.9 %collective-permute-start.13 = (f32[2,32,8,128]{3,2,1,0:T(8,128)S(1)}, f32[2,32,8,128]{3,2,1,0:T(8,128)S(1)}, u32[]{:S(2)}, u32[]{:S(2)}) collective-permute-start(f32[2,32,8,128]{3,2,1,0:T(8,128)S(1)} %get-tuple-element.25), channel_id=1, source_target_pairs={{0,1},{1,2},{2,3},{3,4},{4,5},{5,6},{6,7},{8,9},{9,10},{10,11},{11... | collective-permute-start | bytes 786440 | tf_op jit(solution)/shard_map/source_halo/ppermute | solution.py:276
  171.2 22.2 %collective-permute-start.14 = (f32[2,32,8,128]{3,2,1,0:T(8,128)S(1)}, f32[2,32,8,128]{3,2,1,0:T(8,128)S(1)}, u32[]{:S(2)}, u32[]{:S(2)}) collective-permute-start(f32[2,32,8,128]{3,2,1,0:T(8,128)S(1)} %get-tuple-element.24), channel_id=1, source_target_pairs={{1,0},{2,1},{3,2},{4,3},{5,4},{6,5},{7,6},{9,8},{10,9},{11,10},{12... | collective-permute-start | bytes 786440 | tf_op jit(solution)/shard_map/source_halo/ppermute | solution.py:277

commit v2 on v1

--- a/solution.py
+++ b/solution.py
@@ -44,17 +44,16 @@
     return high, (x - high.astype(f32)).astype(bf16)
 
 
-def rank_kernel(shift_ref, owner_ref, line_ref, slot_ref, label_ref, carry_ref):
-    carry_ref[...] = jnp.zeros_like(carry_ref)
-    label_ref[...] = jnp.zeros_like(label_ref)
+def rank_kernel(shift_ref, owner_ref, line_ref, slot_ref, label_ref):
     rows = lax.broadcasted_iota(jnp.int32, (CHUNK, CHUNK), 0)
     cols = lax.broadcasted_iota(jnp.int32, (CHUNK, CHUNK), 1)
     earlier = jnp.where(rows < cols, 1.0, 0.0).astype(bf16)
     places = lax.broadcasted_iota(jnp.int32, (LANES, CHUNK), 0)
     shift = shift_ref[0]
-
-    def body(c, _):
-        owner = owner_ref[pl.ds(c, 1), :]
+    carry = jnp.zeros((CHUNK, 1), f32)
+    labels = jnp.zeros((CHUNK, LANES), f32)
+    for c in range(0, owner_ref.shape[1], CHUNK):
+        owner = owner_ref[:, c : c + CHUNK]
         fluid, sx, sy = owner >> 6, (owner >> 3) & 7, owner & 7
         peer = (fluid * 2 + (sx & 1)) * 8 + sy
         quad = sx >> 1
@@ -62,16 +61,14 @@
         hit = jnp.where(match, 1.0, 0.0)
         hit16 = hit.astype(bf16)
         before = jnp.dot(hit16, earlier, preferred_element_type=f32)
-        rank = jnp.sum(jnp.where(match, before + carry_ref[...], 0.0), axis=0, keepdims=True)
-        carry_ref[...] += before[:, CHUNK - 1 :] + hit[:, CHUNK - 1 :]
+        rank = jnp.sum(jnp.where(match, before + carry, 0.0), axis=0, keepdims=True)
+        carry = carry + (before[:, CHUNK - 1 :] + hit[:, CHUNK - 1 :])
         rank = rank.astype(jnp.int32)
-        slot_ref[pl.ds(c, 1), :] = peer * PEER_ROWS + quad * SLOTS + rank
-        value = (line_ref[pl.ds(c, 1), :] + 1).astype(f32)
+        slot_ref[:, c : c + CHUNK] = peer * PEER_ROWS + quad * SLOTS + rank
+        value = (line_ref[:, c : c + CHUNK] + 1).astype(f32)
         spread = jnp.where(places == rank + shift, value, 0.0).astype(bf16)
-        label_ref[...] += dot_nt(hit16, spread)
-        return 0
-
-    lax.fori_loop(0, owner_ref.shape[0], body, 0)
+        labels = labels + dot_nt(hit16, spread)
+    label_ref[...] = labels
 
 
 def pack_kernel(slot_ref, blocks_ref, label_ref, out_ref):
@@ -87,53 +84,43 @@
             at = (2 * h + e) * PEER_ROWS + QUADS * SLOTS
             out_ref[at : at + QUADS, :] = label_ref[8 * h + 4 * e : 8 * h + 4 * e + 4, :]
 
-    step = 32
-    per_row = slot_ref.shape[1] // step
+    step = 64
 
     def place(i, _):
-        row, col = i // per_row, (i % per_row) * step
+        base = pl.multiple_of(i * step, step)
         for t in range(step):
-            slot = slot_ref[row, col + t]
-            out_ref[pl.ds(slot, 1), :] = blocks_ref[pl.ds(i * step + t, 1), :]
+            out_ref[pl.ds(slot_ref[0, base + t], 1), :] = blocks_ref[pl.ds(base + t, 1), :]
         return 0
 
     lax.fori_loop(0, blocks_ref.shape[0] // step, place, 0)
 
 
-def deposit_kernel(quad_ref, block_ref, map_ref, *rest):
-    outs, total = rest[:QUADS], rest[QUADS]
-    g = pl.program_id(0)
-
-    @pl.when(g == 0)
-    def _():
-        total[...] = jnp.zeros_like(total)
-
+def deposit_kernel(ahead, quad_ref, block_ref, label_ref, map_ref, out_ref):
+    quad = (quad_ref[0] + ahead) % QUADS
     lines = lax.broadcasted_iota(jnp.int32, (LINES, LANES), 0).astype(f32) + 1.0
-    for q in range(QUADS):
-        marks = []
-        for half in range(2):
-            at = QUADS * SLOTS + q
-            label = block_ref[4 * half, at : at + 1, :]
-            for t in range(1, 4):
-                label = label + block_ref[4 * half + t, at : at + 1, :]
-            marks.append(jnp.where(lines == label, 1.0, 0.0).astype(bf16))
-        mark = jnp.concatenate(marks, axis=1)
-        values = block_ref[:, q * SLOTS : (q + 1) * SLOTS, :].reshape(8 * SLOTS, LANES)
-        high, low = split(values)
-        total[q] += jnp.dot(
-            mark, jnp.concatenate([high, low], axis=1), preferred_element_type=f32
+    labels = label_ref[:, pl.ds(quad, 1), :].reshape(PEERS // 4, 4, LANES).sum(axis=1)
+    total = jnp.zeros((LINES, 2 * LANES), f32)
+    for g in range(PEERS // 8):
+        marks = [
+            jnp.where(lines == labels[h : h + 1], 1.0, 0.0).astype(bf16)
+            for h in (2 * g, 2 * g + 1)
+        ]
+        high, low = split(block_ref[8 * g : 8 * g + 8].reshape(8 * SLOTS, LANES))
+        total = total + jnp.dot(
+            jnp.concatenate(marks, axis=1),
+            jnp.concatenate([high, low], axis=1),
+            preferred_element_type=f32,
         )
-
-    @pl.when(g == pl.num_programs(0) - 1)
-    def _():
-        for k in range(QUADS):
-            both = total[(quad_ref[0] + k) % QUADS]
-            outs[k][...] = source_gain * jnp.dot(
-                both[:, :LANES] + both[:, LANES:],
-                map_ref[...],
-                precision=lax.Precision.HIGHEST,
-                preferred_element_type=f32,
-            )
+    high, low = split(total[:, :LANES] + total[:, LANES:])
+    map_high, map_low = split(map_ref[...])
+    both = jnp.concatenate([map_high, map_low], axis=1)
+    once = jnp.concatenate([map_high, jnp.zeros_like(map_low)], axis=1)
+    mapped = jnp.dot(
+        jnp.concatenate([high, low], axis=1),
+        jnp.concatenate([both, once], axis=0),
+        preferred_element_type=f32,
+    )
+    out_ref[...] = source_gain * (mapped[:, :LANES] + mapped[:, LANES:])
 
 
 def step_kernel(
@@ -180,8 +167,8 @@
     first, last = lane == 0, lane == LANES - 1
 
     def advance(a_m, a_e, b_m, b_e, s):
-        def body(x, _):
-            r = pl.multiple_of(x * WIDE, 8)
+        for x in range(s + 1, WIDE - 1 - s):
+            r = x * WIDE
             at = lambda off: pl.ds(r + pad + off, WIDE)
             own = pl.ds(r, WIDE)
             m, e = a_m[at(0), :], a_e[at(0), :]
@@ -195,9 +182,6 @@
                 beside = beside + (a[at(-WIDE), :] + a[at(WIDE), :])
                 beside = beside + (a[at(-1), :] + a[at(1), :])
                 b[at(0), :] = v + start_ref[d, own, :] * (beside - 6.0 * v) + src[own, :]
-            return 0
-
-        lax.fori_loop(s + 1, WIDE - 1 - s, body, 0)
         for x in range(TILE):
             r = pad + (x + HALO) * WIDE + HALO
             for h in range(2):
@@ -217,11 +201,11 @@
     acc[...] = jnp.zeros_like(acc)
     tall = 8 * HIST
 
-    def gram(i, _):
+    for i in range(TILE):
         x, h = (i // 2) * 2, i % 2
         new = [snaps[(x + e) * 2 + h] for e in range(2)]
         old = [
-            past[:, x + e, pl.ds(pl.multiple_of(h * 8, 8), 8), :].reshape(tall, LANES)
+            past[:, x + e, h * 8 : h * 8 + 8, :].reshape(tall, LANES)
             for e in range(2)
         ]
         new_high, new_low = split(jnp.concatenate(new, axis=1))
@@ -229,9 +213,6 @@
         right = jnp.concatenate([new_high, new_low], axis=0)
         acc[0:tall, :] += dot_nt(old_high, right) + dot_nt(old_low, right)
         acc[tall:, :] += dot_nt(new_high, right) + dot_nt(new_low, right)
-        return 0
-
-    lax.fori_loop(0, TILE, gram, 0)
     y = lax.broadcasted_iota(jnp.int32, acc.shape, 0) % 8
     y_new = lax.broadcasted_iota(jnp.int32, acc.shape, 1) % 8
     products = jnp.where(y == y_new, acc[...], 0.0).reshape(SNAPS, 8, 2 * 8 * STEPS).sum(axis=1)
@@ -292,7 +273,6 @@
     piece_to_solid_line_mapping,
 ):
     blocks = boundary_heat_rate_pieces.shape[0]
-    chunks = blocks // CHUNK
     vmem = pl.BlockSpec(memory_space=pltpu.VMEM)
     smem = pl.BlockSpec(memory_space=pltpu.SMEM)
     limit = pltpu.CompilerParams(vmem_limit_bytes=48 * 1024 * 1024)
@@ -302,18 +282,13 @@
         slots, labels = pl.pallas_call(
             rank_kernel,
             out_shape=(
-                jax.ShapeDtypeStruct((chunks, CHUNK), jnp.int32),
+                jax.ShapeDtypeStruct((1, blocks), jnp.int32),
                 jax.ShapeDtypeStruct((CHUNK, LANES), f32),
             ),
             in_specs=[smem, vmem, vmem],
             out_specs=(vmem, vmem),
-            scratch_shapes=[pltpu.VMEM((CHUNK, 1), f32)],
             compiler_params=limit,
-        )(
-            shift,
-            receiving_processor_per_piece.reshape(chunks, CHUNK),
-            boundary_line_position_in_tile.reshape(chunks, CHUNK),
-        )
+        )(shift, receiving_processor_per_piece.T, boundary_line_position_in_tile.T)
 
     with jax.named_scope("pack"):
         packed = pl.pallas_call(
@@ -324,47 +299,56 @@
             compiler_params=limit,
         )(slots, boundary_heat_rate_pieces, labels)
 
-    with jax.named_scope("early_halo"):
-        pair = jnp.stack([opening_conductor_warmth, rate_step * cellwise_diffusivity])
-        pair = jnp.concatenate([pair, beyond(pair)])
-        _, _, tall, left, right = slabs(pair)
-        start = jnp.concatenate([left, tall, right], axis=2).reshape(4, WIDE * WIDE, LANES)
-        packed, start = lax.optimization_barrier((packed, start))
-
     with jax.named_scope("exchange"):
+        packed, states = lax.optimization_barrier((packed, previous_thermal_states))
         received = lax.all_to_all(
             packed.reshape(PEERS, PEER_ROWS, LANES), PLANE, split_axis=0, concat_axis=0, tiled=True
         )
 
     with jax.named_scope("history"):
-        flat = previous_thermal_states.reshape(HIST, -1)
+        flat = states.reshape(HIST, -1)
         cells = float(flat.shape[1] * lax.axis_size(ALL))
         past_gram = jnp.dot(
             flat, flat.T, precision=lax.Precision.HIGHEST, preferred_element_type=f32
         )
         past_gram = jnp.pad(past_gram, ((0, 0), (0, STEPS)))
 
+    with jax.named_scope("early_halo"):
+        past_gram, pair = lax.optimization_barrier((past_gram, opening_conductor_warmth))
+        pair = jnp.stack([pair, rate_step * cellwise_diffusivity])
+        pair = jnp.concatenate([pair, beyond(pair)])
+        _, _, tall, left, right = slabs(pair)
+        start = jnp.concatenate([left, tall, right], axis=2).reshape(4, WIDE * WIDE, LANES)
+
     with jax.named_scope("deposit"):
-        part = jax.ShapeDtypeStruct((LINES, LANES), f32)
-        parts = pl.pallas_call(
-            deposit_kernel,
-            out_shape=(part,) * QUADS,
-            grid_spec=pltpu.PrefetchScalarGridSpec(
-                num_scalar_prefetch=1,
-                grid=(PEERS // 8,),
-                in_specs=[
-                    pl.BlockSpec((8, PEER_ROWS, LANES), lambda g, _: (g, 0, 0)),
-                    whole((LANES, LANES)),
-                ],
-                out_specs=(whole((LINES, LANES)),) * QUADS,
-                scratch_shapes=[pltpu.VMEM((QUADS, LINES, 2 * LANES), f32)],
-            ),
-            compiler_params=limit,
-        )(lax.axis_index("sxq").astype(jnp.int32).reshape(1), received, piece_to_solid_line_mapping)
-        source = parts[0]
-        for k in range(1, QUADS):
-            ring = [(i, (i + k) % QUADS) for i in range(QUADS)]
-            source = source + lax.ppermute(parts[k], "sxq", ring)
+        received, past_gram = lax.optimization_barrier((received, past_gram))
+        mine = lax.axis_index("sxq").astype(jnp.int32).reshape(1)
+
+        def deposit(ahead):
+            return pl.pallas_call(
+                functools.partial(deposit_kernel, ahead),
+                out_shape=jax.ShapeDtypeStruct((LINES, LANES), f32),
+                grid_spec=pltpu.PrefetchScalarGridSpec(
+                    num_scalar_prefetch=1,
+                    grid=(1,),
+                    in_specs=[
+                        pl.BlockSpec(
+                            (PEERS, SLOTS, LANES), lambda _, quad: (0, (quad[0] + ahead) % QUADS, 0)
+                        ),
+                        pl.BlockSpec((PEERS, 8, LANES), lambda _, quad: (0, QUADS * SLOTS // 8, 0)),
+                        whole((LANES, LANES)),
+                    ],
+                    out_specs=whole((LINES, LANES)),
+                ),
+                compiler_params=limit,
+            )(mine, received, received, piece_to_solid_line_mapping)
+
+        source = None
+        for k in (2, 1, 3, 0):
+            part = deposit(k)
+            if k:
+                part = lax.ppermute(part, "sxq", [(i, (i + k) % QUADS) for i in range(QUADS)])
+            source = part if source is None else source + part
         source = source.reshape(1, TILE, TILE, LANES)
 
     with jax.named_scope("source_halo"):

time: 243 us -> 174 us (0.72)
  waiting for transfers between devices: 79.1 us -> 48.3 us
  Pallas kernels: 51.2 us -> 23.4 us
  other arithmetic: 6.63 us -> 1.31 us
  starting transfers between devices: 57.9 us -> 53.5 us
    all_to_all x1, waiting for transfers between devices: 56.6 us -> 0.01 us  [local(): lax.all_to_all(packed.reshape(PEERS, PEER_ROWS, LANES), PLANE, split_axis...]
    ppermute x2, waiting for transfers between devices: 3.18 us -> 30.6 us  [beyond(): after = lax.ppermute(cells, 'fluid', down_chain('fluid'))]
    pallas_call x1, Pallas kernels: 22.9 us -> 6.9 us  [local(): pl.pallas_call(step_kernel, out_shape=(jax.ShapeDtypeStruct((TILE, TILE,...]
    pallas_call x1, Pallas kernels: 14.4 us -> 6.87 us  [local(): pl.pallas_call(pack_kernel, out_shape=jax.ShapeDtypeStruct((PEERS * PEER_...]
    ppermute x2, waiting for transfers between devices: 0.01 us -> 4.4 us  [slabs(): right = lax.ppermute(tall[:, :, :HALO], 'sy', down_chain('sy'))]
    pallas_call x2 -> x5, Pallas kernels: 13.9 us -> 9.6 us  [the longest x4 7.59 us: deposit(): pl.pallas_call(functools.partial(deposit_kernel, ahead), out_shape=jax.Sh...]
    ppermute x2, waiting for transfers between devices: 3.27 us -> 0.01 us  [beyond(): before = lax.ppermute(cells, 'fluid', up_chain('fluid'))]
    ppermute x2, starting transfers between devices: 7.69 us -> 4.55 us  [slabs(): right = lax.ppermute(tall[:, :, :HALO], 'sy', down_chain('sy'))]
  transfers between devices with their start and end apart: 16 -> 16, of which waited for: 10 -> 8; matrix products, arithmetic and copies ran while one was open for 9% -> 12% of each run, Pallas kernels for 9% -> 4%
where the time goes in v2:
time: 174 us
  starting transfers between devices  53.5 us (31%)
  waiting for transfers between devices  48.3 us (28%)
  Pallas kernels  23.4 us (13%)
  blocking collectives  23.3 us (13%)
  matrix products  19.5 us (11%)
  local copies, waits for them, and re-layouts  3.19 us (2%)
    ppermute x2, waiting for transfers between devices, beyond(): after = lax.ppermute(cells, 'fluid', down_chain('fluid'))  30.6 us
    all_to_all x1, blocking collectives, local(): lax.all_to_all(gram_rows, ALL, split_axis=0, concat_axis=0, tiled=True)  23.3 us
    dot_general x1, matrix products, local(): jnp.dot(flat, flat.T, precision=lax.Precision.HIGHEST, preferred_element_...  19.5 us
    all_to_all x1, starting transfers between devices, local(): lax.all_to_all(packed.reshape(PEERS, PEER_ROWS, LANES), PLANE, split_axis...  10.5 us
    ppermute x3, starting transfers between devices, local(): lax.ppermute(part, 'sxq', [(i, (i + k) % QUADS) for i in range(QUADS)])  10.3 us
    ppermute x2, starting transfers between devices, slabs(): up = lax.ppermute(cells[:, TILE - HALO:], SX, up_chain(SX))  9.54 us
    ppermute x3, waiting for transfers between devices, local(): lax.ppermute(part, 'sxq', [(i, (i + k) % QUADS) for i in range(QUADS)])  8.02 us
    pallas_call x4, Pallas kernels, deposit(): pl.pallas_call(functools.partial(deposit_kernel, ahead), out_shape=jax.Sh...  7.59 us
  transfers between devices with their start and end apart: 16, of which 8 were waited for; matrix products, arithmetic and copies ran while one was open for 12% of the time, Pallas kernels for 4%

profile of v2, /device:TPU:1, one launch (start us, length us, event | category | flops | bytes accessed | tf_op | source)
XLA Modules:
  0.0 173.5 jit_solution(13112492129763091773)
XLA Ops:
  2.1 2.0 %rank.1 = (s32[1,4096]{1,0:T(1,128)S(1)}, f32[256,128]{1,0:T(8,128)S(1)}) custom-call(s32[1]{0:T(128)} %bitcast.shift_ref, s32[1,4096]{1,0:T(1,128)S(1)} %bitcast.21, s32[1,4096]{1,0:T(1,128)S(1)} %bitcast.22), custom_call_target="tpu_custom_call" | custom-call | tf_op jit(solution)/shard_map/rank/pallas_call | solution.py:282
  4.1 1.6 copy-done
  5.7 6.9 %pack.1 = f32[8704,128]{1,0:T(8,128)} custom-call(s32[1,4096]{1,0:T(1,128)S(1)} %get-tuple-element.12.slot_ref, f32[4096,128]{1,0:T(8,128)S(1)} %copy-done, f32[256,128]{1,0:T(8,128)S(1)} %get-tuple-element.13.label_ref), custom_call_target="tpu_custom_call" | custom-call | tf_op jit(solution)/shard_map/pack/pallas_call | solution.py:294
  12.6 10.5 %all-to-all-start = ((f32[64,136,128]{2,1,0:T(8,128)}), f32[64,136,128]{2,1,0:T(8,128)}, u32[]{:S(2)}, u32[]{:S(2)}) async-start(f32[64,136,128]{2,1,0:T(8,128)} %bitcast.23), calls=%async_computation | async-start | bytes 8912896 | tf_op jit(solution)/shard_map/exchange/all_to_all | solution.py:304
  23.1 19.5 %fusion.2 = f32[56,56]{1,0:T(8,128)S(1)} fusion(f32[56,16,16,128]{3,2,1,0:T(8,128)} %history.1), kind=kOutput, calls=%fused_computation.3 | convolution fusion | flops 1233125376 | bytes 7352576 | tf_op jit(solution)/shard_map/history/dot_general | solution.py:311
  42.7 1.3 collective-permute-start
  44.0 4.0 %collective-permute-start.1 = (f32[2,16,16,128]{3,2,1,0:T(8,128)S(1)}, f32[2,16,16,128]{3,2,1,0:T(8,128)S(1)}, u32[]{:S(2)}, u32[]{:S(2)}) collective-permute-start(f32[2,16,16,128]{3,2,1,0:T(8,128)S(1)} %pad_maximum_fusion.5), channel_id=1, source_target_pairs={{0,64},{64,128},{128,192},{1,65},{65,129},{129,193},{2,66},{66,130... | collective-permute-start | bytes 786440 | tf_op jit(solution)/shard_map/early_halo/ppermute | solution.py:248
  48.0 30.3 %collective-permute-done = f32[2,16,16,128]{3,2,1,0:T(8,128)S(1)} collective-permute-done((f32[2,16,16,128]{3,2,1,0:T(8,128)S(1)}, f32[2,16,16,128]{3,2,1,0:T(8,128)S(1)}, u32[]{:S(2)}, u32[]{:S(2)}) %collective-permute-start) | collective-permute-done | bytes 262176 | tf_op jit(solution)/shard_map/early_halo/ppermute | solution.py:247
  78.4 7.5 %collective-permute-start.2 = (f32[4,8,16,128]{3,2,1,0:T(8,128)S(1)}, f32[4,8,16,128]{3,2,1,0:T(8,128)S(1)}, u32[]{:S(2)}, u32[]{:S(2)}) collective-permute-start(f32[4,8,16,128]{3,2,1,0:T(8,128)S(1)} %get-tuple-element.26), channel_id=1, source_target_pairs={{0,8},{8,16},{16,24},{24,32},{32,40},{40,48},{48,56},{1,9},{9,17},... | collective-permute-start | bytes 786440 | tf_op jit(solution)/shard_map/early_halo/ppermute | solution.py:254
  86.0 1.3 collective-permute-start.3
  87.3 1.9 %deposit.4 = f32[256,128]{1,0:T(8,128)S(1)} custom-call(s32[1]{0:T(128)} %bitcast.8.quad_ref, f32[64,136,128]{2,1,0:T(8,128)} %all-to-all-done.block_ref.label_ref, f32[64,136,128]{2,1,0:T(8,128)} %all-to-all-done.block_ref.label_ref, f32[128,128]{1,0:T(8,128)S(1)} %copy-done.1), custom_call_target="tpu_custom_call" | custom-call | tf_op jit(solution)/shard_map/deposit/pallas_call | solution.py:328
  89.2 1.9 %deposit.5 = f32[256,128]{1,0:T(8,128)S(1)} custom-call(s32[1]{0:T(128)} %bitcast.8.quad_ref, f32[64,136,128]{2,1,0:T(8,128)} %all-to-all-done.block_ref.label_ref, f32[64,136,128]{2,1,0:T(8,128)} %all-to-all-done.block_ref.label_ref, f32[128,128]{1,0:T(8,128)S(1)} %copy-done.1), custom_call_target="tpu_custom_call" | custom-call | tf_op jit(solution)/shard_map/deposit/pallas_call | solution.py:328
  91.1 1.9 %deposit.6 = f32[256,128]{1,0:T(8,128)S(1)} custom-call(s32[1]{0:T(128)} %bitcast.8.quad_ref, f32[64,136,128]{2,1,0:T(8,128)} %all-to-all-done.block_ref.label_ref, f32[64,136,128]{2,1,0:T(8,128)} %all-to-all-done.block_ref.label_ref, f32[128,128]{1,0:T(8,128)S(1)} %copy-done.1), custom_call_target="tpu_custom_call" | custom-call | tf_op jit(solution)/shard_map/deposit/pallas_call | solution.py:328
  93.0 6.7 %collective-permute-start.6 = (f32[256,128]{1,0:T(8,128)S(1)}, f32[256,128]{1,0:T(8,128)S(1)}, u32[]{:S(2)}, u32[]{:S(2)}) collective-permute-start(f32[256,128]{1,0:T(8,128)S(1)} %deposit.4), channel_id=1, source_target_pairs={{0,32},{16,48},{32,0},{48,16},{1,33},{17,49},{33,1},{49,17},{2,34}... | collective-permute-start | bytes 393224 | tf_op jit(solution)/shard_map/deposit/ppermute | solution.py:350
  99.7 1.2 collective-permute-start.7
  100.9 2.4 %collective-permute-start.8 = (f32[256,128]{1,0:T(8,128)S(1)}, f32[256,128]{1,0:T(8,128)S(1)}, u32[]{:S(2)}, u32[]{:S(2)}) collective-permute-start(f32[256,128]{1,0:T(8,128)S(1)} %deposit.6), channel_id=1, source_target_pairs={{0,48},{16,0},{32,16},{48,32},{1,49},{17,1},{33,17},{49,33},{2,50}... | collective-permute-start | bytes 393224 | tf_op jit(solution)/shard_map/deposit/ppermute | solution.py:350
  103.4 1.9 %deposit.7 = f32[256,128]{1,0:T(8,128)S(1)} custom-call(s32[1]{0:T(128)} %bitcast.8.quad_ref, f32[64,136,128]{2,1,0:T(8,128)} %all-to-all-done.block_ref.label_ref, f32[64,136,128]{2,1,0:T(8,128)} %all-to-all-done.block_ref.label_ref, f32[128,128]{1,0:T(8,128)S(1)} %copy-done.1), custom_call_target="tpu_custom_call" | custom-call | tf_op jit(solution)/shard_map/deposit/pallas_call | solution.py:328
  105.3 5.7 %collective-permute-done.7 = f32[256,128]{1,0:T(8,128)S(1)} collective-permute-done((f32[256,128]{1,0:T(8,128)S(1)}, f32[256,128]{1,0:T(8,128)S(1)}, u32[]{:S(2)}, u32[]{:S(2)}) %collective-permute-start.7) | collective-permute-done | bytes 131104 | tf_op jit(solution)/shard_map/deposit/ppermute | solution.py:350
  111.0 2.3 %collective-permute-done.8 = f32[256,128]{1,0:T(8,128)S(1)} collective-permute-done((f32[256,128]{1,0:T(8,128)S(1)}, f32[256,128]{1,0:T(8,128)S(1)}, u32[]{:S(2)}, u32[]{:S(2)}) %collective-permute-start.8) | collective-permute-done | bytes 131104 | tf_op jit(solution)/shard_map/deposit/ppermute | solution.py:350
  113.4 3.3 %collective-permute-start.10 = (f32[1,16,16,128]{3,2,1,0:T(8,128)S(1)}, f32[1,16,16,128]{3,2,1,0:T(8,128)S(1)}, u32[]{:S(2)}, u32[]{:S(2)}) collective-permute-start(f32[1,16,16,128]{3,2,1,0:T(8,128)S(1)} %bitcast.28), channel_id=1, source_target_pairs={{0,64},{64,128},{128,192},{1,65},{65,129},{129,193},{2,66},{66,130... | collective-permute-start | bytes 393224 | tf_op jit(solution)/shard_map/source_halo/ppermute | solution.py:248
  116.7 1.3 collective-permute-start.9
  118.0 1.9 %collective-permute-start.4 = (f32[4,32,8,128]{3,2,1,0:T(8,128)S(1)}, f32[4,32,8,128]{3,2,1,0:T(8,128)S(1)}, u32[]{:S(2)}, u32[]{:S(2)}) collective-permute-start(f32[4,32,8,128]{3,2,1,0:T(8,128)S(1)} %get-tuple-element.22), channel_id=1, source_target_pairs={{0,1},{1,2},{2,3},{3,4},{4,5},{5,6},{6,7},{8,9},{9,10},{10,11},{11... | collective-permute-start | bytes 1572872 | tf_op jit(solution)/shard_map/early_halo/ppermute | solution.py:257
  120.0 2.4 %collective-permute-start.5 = (f32[4,32,8,128]{3,2,1,0:T(8,128)S(1)}, f32[4,32,8,128]{3,2,1,0:T(8,128)S(1)}, u32[]{:S(2)}, u32[]{:S(2)}) collective-permute-start(f32[4,32,8,128]{3,2,1,0:T(8,128)S(1)} %get-tuple-element.23), channel_id=1, source_target_pairs={{1,0},{2,1},{3,2},{4,3},{5,4},{6,5},{7,6},{9,8},{10,9},{11,10},{12... | collective-permute-start | bytes 1572872 | tf_op jit(solution)/shard_map/early_halo/ppermute | solution.py:258
  122.8 2.0 %collective-permute-start.11 = (f32[2,8,16,128]{3,2,1,0:T(8,128)S(1)}, f32[2,8,16,128]{3,2,1,0:T(8,128)S(1)}, u32[]{:S(2)}, u32[]{:S(2)}) collective-permute-start(f32[2,8,16,128]{3,2,1,0:T(8,128)S(1)} %get-tuple-element.29), channel_id=1, source_target_pairs={{0,8},{8,16},{16,24},{24,32},{32,40},{40,48},{48,56},{1,9},{9,17},... | collective-permute-start | bytes 393224 | tf_op jit(solution)/shard_map/source_halo/ppermute | solution.py:254
  124.8 1.3 collective-permute-start.12
  126.7 3.8 %collective-permute-done.12.source_down = f32[2,8,16,128]{3,2,1,0:T(8,128)S(1)} collective-permute-done((f32[2,8,16,128]{3,2,1,0:T(8,128)S(1)}, f32[2,8,16,128]{3,2,1,0:T(8,128)S(1)}, u32[]{:S(2)}, u32[]{:S(2)}) %collective-permute-start.12) | collective-permute-done | bytes 131104 | tf_op jit(solution)/shard_map/source_halo/ppermute | solution.py:255
  130.6 4.2 %collective-permute-start.13 = (f32[2,32,8,128]{3,2,1,0:T(8,128)S(1)}, f32[2,32,8,128]{3,2,1,0:T(8,128)S(1)}, u32[]{:S(2)}, u32[]{:S(2)}) collective-permute-start(f32[2,32,8,128]{3,2,1,0:T(8,128)S(1)} %get-tuple-element.25), channel_id=1, source_target_pairs={{0,1},{1,2},{2,3},{3,4},{4,5},{5,6},{6,7},{8,9},{9,10},{10,11},{11... | collective-permute-start | bytes 786440 | tf_op jit(solution)/shard_map/source_halo/ppermute | solution.py:257
  134.8 2.1 %collective-permute-start.14 = (f32[2,32,8,128]{3,2,1,0:T(8,128)S(1)}, f32[2,32,8,128]{3,2,1,0:T(8,128)S(1)}, u32[]{:S(2)}, u32[]{:S(2)}) collective-permute-start(f32[2,32,8,128]{3,2,1,0:T(8,128)S(1)} %get-tuple-element.24), channel_id=1, source_target_pairs={{1,0},{2,1},{3,2},{4,3},{5,4},{6,5},{7,6},{9,8},{10,9},{11,10},{12... | collective-permute-start | bytes 786440 | tf_op jit(solution)/shard_map/source_halo/ppermute | solution.py:258
  137.2 0.9 collective-permute-done.13.source_left
  138.1 4.4 %collective-permute-done.14.source_right = f32[2,32,8,128]{3,2,1,0:T(8,128)S(1)} collective-permute-done((f32[2,32,8,128]{3,2,1,0:T(8,128)S(1)}, f32[2,32,8,128]{3,2,1,0:T(8,128)S(1)}, u32[]{:S(2)}, u32[]{:S(2)}) %collective-permute-start.14) | collective-permute-done | bytes 262176 | tf_op jit(solution)/shard_map/source_halo/ppermute | solution.py:258
  142.5 6.9 %steps.1 = (f32[16,16,128]{2,1,0:T(8,128)}, f32[256,64]{1,0:T(8,128)S(1)}) custom-call(f32[4,1024,128]{2,1,0:T(8,128)S(1)} %bitcast.19, f32[2,16,16,128]{3,2,1,0:T(8,128)S(1)} %pad_maximum_fusion.4.source_ref, f32[2,8,16,128]{3,2,1,0:T(8,128)S(1)} %collective-permute-done.11.source_up, f32[2,8,16,128]{3,2,1,0:T(8,128)S(1)} %collective-permute-done.12.source_down, ...), custom_call_target="tpu_custom_call" | custom-call | tf_op jit(solution)/shard_map/steps/pallas_call | solution.py:362
  149.4 23.3 %all_to_all.14 = f32[256,1,64]{2,1,0:T(1,128)S(1)} all-to-all(f32[256,1,64]{2,1,0:T(1,128)S(1)} %bitcast.20), channel_id=1, replica_groups=mesh['fluid'=4,'sxq'=4,'sxp'=2,'sy'=8] {'fluid','sxq','sxp','sy'}, dimensions={0} | all-to-all | bytes 131072 | tf_op jit(solution)/shard_map/gram_sum/all_to_all | solution.py:386
  (39 shorter events, 3.9 us)
Async XLA Ops:
  0.6 0.7 copy-start.2
  1.4 0.7 copy-start.3
  4.1 1.6 copy-start
  12.6 74.7 %all-to-all-start = ((f32[64,136,128]{2,1,0:T(8,128)}), f32[64,136,128]{2,1,0:T(8,128)}, u32[]{:S(2)}, u32[]{:S(2)}) async-start(f32[64,136,128]{2,1,0:T(8,128)} %bitcast.23), calls=%async_computation | async-start | bytes 8912896 | tf_op jit(solution)/shard_map/exchange/all_to_all | solution.py:304
  23.1 19.6 %copy-start.5 = (f32[16,16,128]{2,1,0:T(8,128)S(1)}, f32[16,16,128]{2,1,0:T(8,128)}, u32[]{:S(2)}) copy-start(f32[16,16,128]{2,1,0:T(8,128)} %param.8) | copy-start | bytes 393220
  23.1 19.6 %copy-start.4 = (f32[16,16,128]{2,1,0:T(8,128)S(1)}, f32[16,16,128]{2,1,0:T(8,128)}, u32[]{:S(2)}) copy-start(f32[16,16,128]{2,1,0:T(8,128)} %param.7) | copy-start | bytes 393220
  42.6 44.7 %copy-start.1 = (f32[128,128]{1,0:T(8,128)S(1)}, f32[128,128]{1,0:T(8,128)}, u32[]{:S(2)}) copy-start(f32[128,128]{1,0:T(8,128)} %map_ref.7) | copy-start | bytes 196612
  42.7 35.6 %collective-permute-start = (f32[2,16,16,128]{3,2,1,0:T(8,128)S(1)}, f32[2,16,16,128]{3,2,1,0:T(8,128)S(1)}, u32[]{:S(2)}, u32[]{:S(2)}) collective-permute-start(f32[2,16,16,128]{3,2,1,0:T(8,128)S(1)} %pad_maximum_fusion.5), channel_id=1, source_target_pairs={{64,0},{128,64},{192,128},{65,1},{129,65},{193,129},{66,2},{130,66... | collective-permute-start | bytes 786440 | tf_op jit(solution)/shard_map/early_halo/ppermute | solution.py:247
  44.0 34.3 %collective-permute-start.1 = (f32[2,16,16,128]{3,2,1,0:T(8,128)S(1)}, f32[2,16,16,128]{3,2,1,0:T(8,128)S(1)}, u32[]{:S(2)}, u32[]{:S(2)}) collective-permute-start(f32[2,16,16,128]{3,2,1,0:T(8,128)S(1)} %pad_maximum_fusion.5), channel_id=1, source_target_pairs={{0,64},{64,128},{128,192},{1,65},{65,129},{129,193},{2,66},{66,130... | collective-permute-start | bytes 786440 | tf_op jit(solution)/shard_map/early_halo/ppermute | solution.py:248
  78.4 24.9 %collective-permute-start.2 = (f32[4,8,16,128]{3,2,1,0:T(8,128)S(1)}, f32[4,8,16,128]{3,2,1,0:T(8,128)S(1)}, u32[]{:S(2)}, u32[]{:S(2)}) collective-permute-start(f32[4,8,16,128]{3,2,1,0:T(8,128)S(1)} %get-tuple-element.26), channel_id=1, source_target_pairs={{0,8},{8,16},{16,24},{24,32},{32,40},{40,48},{48,56},{1,9},{9,17},... | collective-permute-start | bytes 786440 | tf_op jit(solution)/shard_map/early_halo/ppermute | solution.py:254
  86.0 17.3 %collective-permute-start.3 = (f32[4,8,16,128]{3,2,1,0:T(8,128)S(1)}, f32[4,8,16,128]{3,2,1,0:T(8,128)S(1)}, u32[]{:S(2)}, u32[]{:S(2)}) collective-permute-start(f32[4,8,16,128]{3,2,1,0:T(8,128)S(1)} %get-tuple-element.27), channel_id=1, source_target_pairs={{8,0},{16,8},{24,16},{32,24},{40,32},{48,40},{56,48},{9,1},{17,9},... | collective-permute-start | bytes 786440 | tf_op jit(solution)/shard_map/early_halo/ppermute | solution.py:255
  93.0 12.3 %collective-permute-start.6 = (f32[256,128]{1,0:T(8,128)S(1)}, f32[256,128]{1,0:T(8,128)S(1)}, u32[]{:S(2)}, u32[]{:S(2)}) collective-permute-start(f32[256,128]{1,0:T(8,128)S(1)} %deposit.4), channel_id=1, source_target_pairs={{0,32},{16,48},{32,0},{48,16},{1,33},{17,49},{33,1},{49,17},{2,34}... | collective-permute-start | bytes 393224 | tf_op jit(solution)/shard_map/deposit/ppermute | solution.py:350
  99.7 11.3 %collective-permute-start.7 = (f32[256,128]{1,0:T(8,128)S(1)}, f32[256,128]{1,0:T(8,128)S(1)}, u32[]{:S(2)}, u32[]{:S(2)}) collective-permute-start(f32[256,128]{1,0:T(8,128)S(1)} %deposit.5), channel_id=1, source_target_pairs={{0,16},{16,32},{32,48},{48,0},{1,17},{17,33},{33,49},{49,1},{2,18}... | collective-permute-start | bytes 393224 | tf_op jit(solution)/shard_map/deposit/ppermute | solution.py:350
  100.9 12.4 %collective-permute-start.8 = (f32[256,128]{1,0:T(8,128)S(1)}, f32[256,128]{1,0:T(8,128)S(1)}, u32[]{:S(2)}, u32[]{:S(2)}) collective-permute-start(f32[256,128]{1,0:T(8,128)S(1)} %deposit.6), channel_id=1, source_target_pairs={{0,48},{16,0},{32,16},{48,32},{1,49},{17,1},{33,17},{49,33},{2,50}... | collective-permute-start | bytes 393224 | tf_op jit(solution)/shard_map/deposit/ppermute | solution.py:350
  113.4 9.0 %collective-permute-start.10 = (f32[1,16,16,128]{3,2,1,0:T(8,128)S(1)}, f32[1,16,16,128]{3,2,1,0:T(8,128)S(1)}, u32[]{:S(2)}, u32[]{:S(2)}) collective-permute-start(f32[1,16,16,128]{3,2,1,0:T(8,128)S(1)} %bitcast.28), channel_id=1, source_target_pairs={{0,64},{64,128},{128,192},{1,65},{65,129},{129,193},{2,66},{66,130... | collective-permute-start | bytes 393224 | tf_op jit(solution)/shard_map/source_halo/ppermute | solution.py:248
  116.7 6.1 %collective-permute-start.9 = (f32[1,16,16,128]{3,2,1,0:T(8,128)S(1)}, f32[1,16,16,128]{3,2,1,0:T(8,128)S(1)}, u32[]{:S(2)}, u32[]{:S(2)}) collective-permute-start(f32[1,16,16,128]{3,2,1,0:T(8,128)S(1)} %bitcast.29), channel_id=1, source_target_pairs={{64,0},{128,64},{192,128},{65,1},{129,65},{193,129},{66,2},{130,66... | collective-permute-start | bytes 393224 | tf_op jit(solution)/shard_map/source_halo/ppermute | solution.py:247
  118.0 18.9 %collective-permute-start.4 = (f32[4,32,8,128]{3,2,1,0:T(8,128)S(1)}, f32[4,32,8,128]{3,2,1,0:T(8,128)S(1)}, u32[]{:S(2)}, u32[]{:S(2)}) collective-permute-start(f32[4,32,8,128]{3,2,1,0:T(8,128)S(1)} %get-tuple-element.22), channel_id=1, source_target_pairs={{0,1},{1,2},{2,3},{3,4},{4,5},{5,6},{6,7},{8,9},{9,10},{10,11},{11... | collective-permute-start | bytes 1572872 | tf_op jit(solution)/shard_map/early_halo/ppermute | solution.py:257
  120.0 17.0 %collective-permute-start.5 = (f32[4,32,8,128]{3,2,1,0:T(8,128)S(1)}, f32[4,32,8,128]{3,2,1,0:T(8,128)S(1)}, u32[]{:S(2)}, u32[]{:S(2)}) collective-permute-start(f32[4,32,8,128]{3,2,1,0:T(8,128)S(1)} %get-tuple-element.23), channel_id=1, source_target_pairs={{1,0},{2,1},{3,2},{4,3},{5,4},{6,5},{7,6},{9,8},{10,9},{11,10},{12... | collective-permute-start | bytes 1572872 | tf_op jit(solution)/shard_map/early_halo/ppermute | solution.py:258
  122.8 3.9 %collective-permute-start.11 = (f32[2,8,16,128]{3,2,1,0:T(8,128)S(1)}, f32[2,8,16,128]{3,2,1,0:T(8,128)S(1)}, u32[]{:S(2)}, u32[]{:S(2)}) collective-permute-start(f32[2,8,16,128]{3,2,1,0:T(8,128)S(1)} %get-tuple-element.29), channel_id=1, source_target_pairs={{0,8},{8,16},{16,24},{24,32},{32,40},{40,48},{48,56},{1,9},{9,17},... | collective-permute-start | bytes 393224 | tf_op jit(solution)/shard_map/source_halo/ppermute | solution.py:254
  124.8 5.7 %collective-permute-start.12 = (f32[2,8,16,128]{3,2,1,0:T(8,128)S(1)}, f32[2,8,16,128]{3,2,1,0:T(8,128)S(1)}, u32[]{:S(2)}, u32[]{:S(2)}) collective-permute-start(f32[2,8,16,128]{3,2,1,0:T(8,128)S(1)} %get-tuple-element.28), channel_id=1, source_target_pairs={{8,0},{16,8},{24,16},{32,24},{40,32},{48,40},{56,48},{9,1},{17,9},... | collective-permute-start | bytes 393224 | tf_op jit(solution)/shard_map/source_halo/ppermute | solution.py:255
  130.6 7.5 %collective-permute-start.13 = (f32[2,32,8,128]{3,2,1,0:T(8,128)S(1)}, f32[2,32,8,128]{3,2,1,0:T(8,128)S(1)}, u32[]{:S(2)}, u32[]{:S(2)}) collective-permute-start(f32[2,32,8,128]{3,2,1,0:T(8,128)S(1)} %get-tuple-element.25), channel_id=1, source_target_pairs={{0,1},{1,2},{2,3},{3,4},{4,5},{5,6},{6,7},{8,9},{9,10},{10,11},{11... | collective-permute-start | bytes 786440 | tf_op jit(solution)/shard_map/source_halo/ppermute | solution.py:257
  134.8 7.7 %collective-permute-start.14 = (f32[2,32,8,128]{3,2,1,0:T(8,128)S(1)}, f32[2,32,8,128]{3,2,1,0:T(8,128)S(1)}, u32[]{:S(2)}, u32[]{:S(2)}) collective-permute-start(f32[2,32,8,128]{3,2,1,0:T(8,128)S(1)} %get-tuple-element.24), channel_id=1, source_target_pairs={{1,0},{2,1},{3,2},{4,3},{5,4},{6,5},{7,6},{9,8},{10,9},{11,10},{12... | collective-permute-start | bytes 786440 | tf_op jit(solution)/shard_map/source_halo/ppermute | solution.py:258

commit v3 on v2

v3 whole, which is shorter than its diff:
```python
import functools

import jax
import jax.numpy as jnp
from jax import lax
from jax.experimental import pallas as pl
from jax.experimental.pallas import tpu as pltpu
from jax.sharding import Mesh
from jax.sharding import PartitionSpec as P

STEPS = 8
HALO = 8
HIST = 56
SNAPS = HIST + STEPS
SLOTS = 32
LINES = 256
LANES = 128
QUADS = 4
PEERS = 64
PEER_ROWS = QUADS * SLOTS + 8
CHUNK = 256
TILE = 16
WIDE = TILE + 2 * HALO

rate_step = 0.16
source_gain = 0.1

SX = ("sxq", "sxp")
PLANE = ("fluid", "sxp", "sy")
ALL = ("fluid", "sxq", "sxp", "sy")

f32 = jnp.float32
bf16 = jnp.bfloat16

LIMIT = pltpu.CompilerParams(vmem_limit_bytes=32 * 1024 * 1024)
FULL = pltpu.CompilerParams(vmem_limit_bytes=60 * 1024 * 1024)


def dot_nt(a, b, precision=None):
    return lax.dot_general(
        a, b, (((1,), (1,)), ((), ())), precision=precision, preferred_element_type=f32
    )


def split(x):
    high = x.astype(bf16)
    return high, (x - high.astype(f32)).astype(bf16)


def pack_kernel(
    shift_ref,
    owner_hbm,
    line_hbm,
    blocks_hbm,
    out_ref,
    owner_ref,
    line_ref,
    blocks_ref,
    slot_ref,
    slot_smem,
    sems,
):
    loads = [
        pltpu.make_async_copy(owner_hbm, owner_ref, sems.at[0]),
        pltpu.make_async_copy(line_hbm, line_ref, sems.at[1]),
        pltpu.make_async_copy(blocks_hbm, blocks_ref, sems.at[2]),
    ]
    for load in loads:
        load.start()
    out_ref[...] = jnp.zeros_like(out_ref)

    rows = lax.broadcasted_iota(jnp.int32, (CHUNK, CHUNK), 0)
    cols = lax.broadcasted_iota(jnp.int32, (CHUNK, CHUNK), 1)
    earlier = jnp.where(rows < cols, 1.0, 0.0).astype(bf16)
    places = lax.broadcasted_iota(jnp.int32, (LANES, CHUNK), 0)
    shift = shift_ref[0]
    carry = jnp.zeros((CHUNK, 1), f32)
    labels = jnp.zeros((CHUNK, LANES), f32)
    loads[0].wait()
    loads[1].wait()
    for c in range(0, owner_ref.shape[1], CHUNK):
        owner = owner_ref[:, c : c + CHUNK]
        fluid, sx, sy = owner >> 6, (owner >> 3) & 7, owner & 7
        peer = (fluid * 2 + (sx & 1)) * 8 + sy
        quad = sx >> 1
        match = rows == peer * QUADS + quad
        hit = jnp.where(match, 1.0, 0.0)
        hit16 = hit.astype(bf16)
        before = jnp.dot(hit16, earlier, preferred_element_type=f32)
        rank = jnp.sum(jnp.where(match, before + carry, 0.0), axis=0, keepdims=True)
        carry = carry + (before[:, CHUNK - 1 :] + hit[:, CHUNK - 1 :])
        rank = rank.astype(jnp.int32)
        slot_ref[:, c : c + CHUNK] = peer * PEER_ROWS + quad * SLOTS + rank
        value = (line_ref[:, c : c + CHUNK] + 1).astype(f32)
        spread = jnp.where(places == rank + shift, value, 0.0).astype(bf16)
        labels = labels + dot_nt(hit16, spread)
    to_smem = pltpu.make_async_copy(slot_ref, slot_smem, sems.at[3])
    to_smem.start()
    for g in range(PEERS):
        at = g * PEER_ROWS + QUADS * SLOTS
        out_ref[at : at + QUADS, :] = labels[QUADS * g : QUADS * (g + 1)]
    to_smem.wait()
    loads[2].wait()

    step = 64

    def place(i, _):
        base = pl.multiple_of(i * step, step)
        for t in range(step):
            out_ref[pl.ds(slot_smem[0, base + t], 1), :] = blocks_ref[pl.ds(base + t, 1), :]
        return 0

    lax.fori_loop(0, blocks_ref.shape[0] // step, place, 0)


def quad_step(ahead, step):
    value = ahead[0]
    for n in range(1, len(ahead)):
        value = jnp.where(step == n, ahead[n], value)
    return value


def deposit_kernel(ahead, quad_ref, block_ref, label_ref, map_ref, *out_refs):
    step = pl.program_id(0)
    quad = (quad_ref[0] + quad_step(ahead, step)) % QUADS
    lines = lax.broadcasted_iota(jnp.int32, (LINES, LANES), 0).astype(f32) + 1.0
    labels = label_ref[:, pl.ds(quad, 1), :].reshape(PEERS // 4, 4, LANES).sum(axis=1)
    total = jnp.zeros((LINES, 2 * LANES), f32)
    for g in range(PEERS // 8):
        marks = [
            jnp.where(lines == labels[h : h + 1], 1.0, 0.0).astype(bf16)
            for h in (2 * g, 2 * g + 1)
        ]
        high, low = split(block_ref[8 * g : 8 * g + 8].reshape(8 * SLOTS, LANES))
        total = total + jnp.dot(
            jnp.concatenate(marks, axis=1),
            jnp.concatenate([high, low], axis=1),
            preferred_element_type=f32,
        )
    high, low = split(total[:, :LANES] + total[:, LANES:])
    map_high, map_low = split(map_ref[...])
    both = jnp.concatenate([map_high, map_low], axis=1)
    once = jnp.concatenate([map_high, jnp.zeros_like(map_low)], axis=1)
    mapped = jnp.dot(
        jnp.concatenate([high, low], axis=1),
        jnp.concatenate([both, once], axis=0),
        preferred_element_type=f32,
    )
    result = source_gain * (mapped[:, :LANES] + mapped[:, LANES:])
    for n, out_ref in enumerate(out_refs):

        @pl.when(step == n)
        def _():
            out_ref[...] = result


def cut_kernel(field_ref, rate_ref, *refs):
    sources, (tile_ref, last_ref, first_ref) = refs[:QUADS], refs[QUADS:]
    source = sources[0][...]
    for ref in sources[1:]:
        source = source + ref[...]
    source = source.reshape(TILE, TILE, LANES)
    for k, value in enumerate((field_ref[...], rate_step * rate_ref[...], source)):
        tile_ref[k] = value
        first_ref[k] = value[:HALO]
        last_ref[k] = value[TILE - HALO :]


def side_kernel(up_ref, tile_ref, down_ref, last_ref, first_ref):
    for at, ref in ((0, up_ref), (HALO, tile_ref), (HALO + TILE, down_ref)):
        rows = slice(at, at + ref.shape[1])
        first_ref[:, rows] = ref[:, :, :HALO, :]
        last_ref[:, rows] = ref[:, :, TILE - HALO :, :]


def widen_kernel(up_ref, tile_ref, down_ref, left_ref, right_ref, wide_ref, low_ref, high_ref):
    for k in range(wide_ref.shape[0]):
        for at, ref in ((0, up_ref), (HALO, tile_ref), (HALO + TILE, down_ref)):
            for n in range(ref.shape[1]):
                x = at + n
                r = x * WIDE
                wide_ref[k, r : r + HALO, :] = left_ref[k, x]
                wide_ref[k, r + HALO : r + HALO + TILE, :] = ref[k, n]
                wide_ref[k, r + HALO + TILE : r + WIDE, :] = right_ref[k, x]
        for r in range(0, WIDE * WIDE, LANES):
            turned = wide_ref[k, r : r + LANES, :].T
            low_ref[k, :, r : r + LANES] = turned[:HALO]
            high_ref[k, :, r : r + LANES] = turned[LANES - HALO :]


def step_kernel(
    wide_ref,
    before_ref,
    after_ref,
    past_gram,
    past,
    field_ref,
    rows_ref,
    now_m,
    now_e,
    next_m,
    next_e,
    rate_e,
    src_e,
    snaps,
    acc,
):
    pad = WIDE
    count = WIDE * WIDE
    for now in (now_m, now_e, next_m, next_e):
        now[...] = jnp.zeros_like(now)
    now_m[pad : pad + count, :] = wide_ref[0]
    none = jnp.zeros((LANES - 2 * HALO, LANES), f32)
    for r in range(0, count, LANES):
        own = slice(r, r + LANES)
        for k, (to, off) in enumerate(((now_e, pad), (rate_e, 0), (src_e, 0))):
            lanes = jnp.concatenate([after_ref[k, :, own], none, before_ref[k, :, own]], axis=0)
            to[off + r : off + r + LANES, :] = lanes.T
    lane = lax.broadcasted_iota(jnp.int32, (WIDE, LANES), 1)
    first, last = lane == 0, lane == LANES - 1

    def advance(a_m, a_e, b_m, b_e, s):
        for x in range(s + 1, WIDE - 1 - s):
            r = x * WIDE
            at = lambda off: pl.ds(r + pad + off, WIDE)
            own = pl.ds(r, WIDE)
            m, e = a_m[at(0), :], a_e[at(0), :]
            roll = lambda v, d: pltpu.roll(v, d % LANES, 1)
            mr, er, ml, el = roll(m, 1), roll(e, 1), roll(m, -1), roll(e, -1)
            sides = (
                (a_m, b_m, m, jnp.where(first, er, mr) + jnp.where(last, el, ml)),
                (a_e, b_e, e, jnp.where(first, mr, er) + jnp.where(last, ml, el)),
            )
            rates = (wide_ref[1, own, :], rate_e[own, :])
            sources = (wide_ref[2, own, :], src_e[own, :])
            for (a, b, v, beside), rate, src in zip(sides, rates, sources):
                beside = beside + (a[at(-WIDE), :] + a[at(WIDE), :])
                beside = beside + (a[at(-1), :] + a[at(1), :])
                b[at(0), :] = v + rate * (beside - 6.0 * v) + src
        for x in range(TILE):
            r = pad + (x + HALO) * WIDE + HALO
            for h in range(2):
                snaps[x * 2 + h, 8 * s : 8 * s + 8, :] = b_m[r + 8 * h : r + 8 * h + 8, :]

    for s in range(0, STEPS, 2):
        advance(now_m, now_e, next_m, next_e, s)
        advance(next_m, next_e, now_m, now_e, s + 1)
    for x in range(TILE):
        for h in range(2):
            field_ref[x, 8 * h : 8 * h + 8, :] = snaps[x * 2 + h, 8 * (STEPS - 1) :, :]

    acc[...] = jnp.zeros_like(acc)
    tall = 8 * HIST

    for i in range(TILE):
        x, h = (i // 2) * 2, i % 2
        new = [snaps[(x + e) * 2 + h] for e in range(2)]
        old = [
            past[:, x + e, h * 8 : h * 8 + 8, :].reshape(tall, LANES)
            for e in range(2)
        ]
        new_high, new_low = split(jnp.concatenate(new, axis=1))
        old_high, old_low = split(jnp.concatenate(old, axis=1))
        right = jnp.concatenate([new_high, new_low], axis=0)
        acc[0:tall, :] += dot_nt(old_high, right) + dot_nt(old_low, right)
        acc[tall:, :] += dot_nt(new_high, right) + dot_nt(new_low, right)
    y = lax.broadcasted_iota(jnp.int32, acc.shape, 0) % 8
    y_new = lax.broadcasted_iota(jnp.int32, acc.shape, 1) % 8
    products = jnp.where(y == y_new, acc[...], 0.0).reshape(SNAPS, 8, 2 * 8 * STEPS).sum(axis=1)
    snap_of = lambda shape, dim: (lax.broadcasted_iota(jnp.int32, shape, dim) % 64) // 8
    wide, tallest = (2 * 8 * STEPS, SNAPS), (STEPS, 2 * 8 * STEPS)
    pick = snap_of(wide, 0) == lax.broadcasted_iota(jnp.int32, wide, 1) - HIST
    right = jnp.dot(
        products,
        jnp.where(pick, 1.0, 0.0),
        precision=lax.Precision.HIGHEST,
        preferred_element_type=f32,
    )
    pick = snap_of(tallest, 1) == lax.broadcasted_iota(jnp.int32, tallest, 0)
    low = dot_nt(jnp.where(pick, 1.0, 0.0), products, lax.Precision.HIGHEST)
    upper = past_gram[...] + right[:HIST]
    for f in range(rows_ref.shape[0] // SNAPS):
        rows_ref[f * SNAPS : f * SNAPS + HIST, :] = upper
        rows_ref[f * SNAPS + HIST : (f + 1) * SNAPS, :] = low


def up_chain(axis):
    count = lax.axis_size(axis)
    return [(i, i + 1) for i in range(count - 1)]


def down_chain(axis):
    count = lax.axis_size(axis)
    return [(i + 1, i) for i in range(count - 1)]


def stack(*shape):
    return jax.ShapeDtypeStruct((3, *shape), f32)


def in_vmem(kernel, out_shape, *args):
    vmem = pl.BlockSpec(memory_space=pltpu.VMEM)
    return pl.pallas_call(
        kernel,
        out_shape=out_shape,
        in_specs=[vmem] * len(args),
        out_specs=[vmem] * len(out_shape),
        compiler_params=LIMIT,
    )(*args)


def widened(field, rate, parts):
    half = stack(HALO, TILE, LANES)
    tile, last, first = in_vmem(
        cut_kernel, (stack(TILE, TILE, LANES), half, half), field, rate, *parts
    )
    up = lax.ppermute(last, SX, up_chain(SX))
    down = lax.ppermute(first, SX, down_chain(SX))
    half = stack(WIDE, HALO, LANES)
    last, first = in_vmem(side_kernel, (half, half), up, tile, down)
    left = lax.ppermute(last, "sy", up_chain("sy"))
    right = lax.ppermute(first, "sy", down_chain("sy"))
    edge = stack(HALO, WIDE * WIDE)
    wide, low, high = in_vmem(
        widen_kernel, (stack(WIDE * WIDE, LANES), edge, edge), up, tile, down, left, right
    )
    before = lax.ppermute(high, "fluid", up_chain("fluid"))
    after = lax.ppermute(low, "fluid", down_chain("fluid"))
    return wide, before, after


def whole(shape):
    return pl.BlockSpec(shape, lambda *_: (0,) * len(shape))


def local(
    opening_conductor_warmth,
    cellwise_diffusivity,
    previous_thermal_states,
    boundary_heat_rate_pieces,
    receiving_processor_per_piece,
    boundary_line_position_in_tile,
    piece_to_solid_line_mapping,
):
    blocks = boundary_heat_rate_pieces.shape[0]
    vmem = pl.BlockSpec(memory_space=pltpu.VMEM)
    smem = pl.BlockSpec(memory_space=pltpu.SMEM)
    hbm = pl.BlockSpec(memory_space=pltpu.HBM)

    with jax.named_scope("pack"):
        shift = (lax.axis_index("sy") % 4 * SLOTS).astype(jnp.int32).reshape(1)
        packed = pl.pallas_call(
            pack_kernel,
            out_shape=jax.ShapeDtypeStruct((PEERS * PEER_ROWS, LANES), f32),
            in_specs=[smem] + [hbm] * 3,
            out_specs=vmem,
            scratch_shapes=[
                pltpu.VMEM((1, blocks), jnp.int32),
                pltpu.VMEM((1, blocks), jnp.int32),
                pltpu.VMEM((blocks, LANES), f32),
                pltpu.VMEM((1, blocks), jnp.int32),
                pltpu.SMEM((1, blocks), jnp.int32),
                pltpu.SemaphoreType.DMA((4,)),
            ],
            compiler_params=FULL,
        )(
            shift,
            receiving_processor_per_piece.T,
            boundary_line_position_in_tile.T,
            boundary_heat_rate_pieces,
        )

    with jax.named_scope("exchange"):
        packed, states = lax.optimization_barrier((packed, previous_thermal_states))
        received = lax.all_to_all(
            packed.reshape(PEERS, PEER_ROWS, LANES), PLANE, split_axis=0, concat_axis=0, tiled=True
        )

    with jax.named_scope("history"):
        flat = states.reshape(HIST, -1)
        cells = float(flat.shape[1] * lax.axis_size(ALL))
        past_gram = jnp.dot(
            flat, flat.T, precision=lax.Precision.HIGHEST, preferred_element_type=f32
        )
        past_gram = jnp.pad(past_gram, ((0, 0), (0, STEPS)))

    with jax.named_scope("deposit"):
        received, past_gram = lax.optimization_barrier((received, past_gram))
        mine = lax.axis_index("sxq").astype(jnp.int32).reshape(1)

        def deposit(*ahead):
            quad_of = lambda step, quad: (quad[0] + quad_step(ahead, step)) % QUADS
            return pl.pallas_call(
                functools.partial(deposit_kernel, ahead),
                out_shape=[jax.ShapeDtypeStruct((LINES, LANES), f32)] * len(ahead),
                grid_spec=pltpu.PrefetchScalarGridSpec(
                    num_scalar_prefetch=1,
                    grid=(len(ahead),),
                    in_specs=[
                        pl.BlockSpec(
                            (PEERS, SLOTS, LANES), lambda step, quad: (0, quad_of(step, quad), 0)
                        ),
                        pl.BlockSpec((PEERS, 8, LANES), lambda *_: (0, QUADS * SLOTS // 8, 0)),
                        whole((LANES, LANES)),
                    ],
                    out_specs=[whole((LINES, LANES))] * len(ahead),
                ),
                compiler_params=LIMIT,
            )(mine, received, received, piece_to_solid_line_mapping)

        ahead = (2, 1, 3)
        parts = [
            lax.ppermute(part, "sxq", [(i, (i + k) % QUADS) for i in range(QUADS)])
            for k, part in zip(ahead, deposit(*ahead))
        ]
        parts = [*deposit(0), *parts]

    with jax.named_scope("halo"):
        wide, before, after = widened(opening_conductor_warmth, cellwise_diffusivity, parts)

    with jax.named_scope("steps"):
        rows = lax.axis_size("fluid") * SNAPS
        grid_rows = WIDE * WIDE
        buffer = pltpu.VMEM((grid_rows + 2 * WIDE, LANES), f32)
        field, gram_rows = pl.pallas_call(
            step_kernel,
            out_shape=(
                jax.ShapeDtypeStruct((TILE, TILE, LANES), f32),
                jax.ShapeDtypeStruct((rows, SNAPS), f32),
            ),
            in_specs=[vmem] * 5,
            out_specs=(vmem, vmem),
            scratch_shapes=[
                buffer,
                buffer,
                buffer,
                buffer,
                pltpu.VMEM((grid_rows, LANES), f32),
                pltpu.VMEM((grid_rows, LANES), f32),
                pltpu.VMEM((TILE * 2, 8 * STEPS, LANES), f32),
                pltpu.VMEM((8 * SNAPS, 2 * 8 * STEPS), f32),
            ],
            compiler_params=LIMIT,
        )(wide, before, after, past_gram, previous_thermal_states)

    with jax.named_scope("gram_sum"):
        shares = lax.all_to_all(gram_rows, ALL, split_axis=0, concat_axis=0, tiled=True)
        inner_product_matrix = jnp.sum(shares, axis=0, keepdims=True) / cells
    return field, inner_product_matrix


def solution(mesh):
    fluid, sx, sy = (mesh.shape[name] for name in ("fluid", "sx", "sy"))
    inner = Mesh(mesh.devices.reshape(fluid, sx // 2, 2, sy), ALL)
    cell = P(SX, "sy", "fluid")
    wall = P(ALL, None)
    return jax.shard_map(
        local,
        mesh=inner,
        in_specs=(cell, cell, P(None, SX, "sy", "fluid"), wall, wall, wall, P()),
        out_specs=(cell, P((*SX, "sy"), None)),
        check_vma=False,
    )
```

time: 174 us -> 160 us (0.920)
  starting transfers between devices: 53.5 us -> 32.9 us
  waiting for transfers between devices: 48.3 us -> 60 us
  local copies, waits for them, and re-layouts: 3.19 us -> 0.03 us
  Pallas kernels: 23.4 us -> 21.2 us
    all_to_all x1, waiting for transfers between devices: 0.01 us -> 37.1 us  [local(): lax.all_to_all(packed.reshape(PEERS, PEER_ROWS, LANES), PLANE, split_axis...]
    ppermute x12 -> x6, waiting for transfers between devices: 40.3 us -> 16.4 us  [the longest x1 4.4 us: widened(): right = lax.ppermute(first, 'sy', down_chain('sy'))]
    ppermute x12 -> x6, starting transfers between devices: 32.7 us -> 12.6 us  [the longest x1 3.08 us: widened(): right = lax.ppermute(first, 'sy', down_chain('sy'))]
    pallas_call x5, Pallas kernels: 9.6 us -> 6.46 us  [the longest x2 5.89 us: deposit(): pl.pallas_call(functools.partial(deposit_kernel, ahead), out_shape=[jax.S...]
    unnamed x12 -> x10, local copies, waits for them, and re-layouts: 3.04 us -> 0.02 us
    pallas_call x1, Pallas kernels: 6.87 us -> 8.93 us  [local(): pl.pallas_call(pack_kernel, out_shape=jax.ShapeDtypeStruct((PEERS * PEER_...]
  transfers between devices with their start and end apart: 16 -> 10, of which waited for: 8 -> 10; matrix products, arithmetic and copies ran while one was open for 12% -> 12% of each run, Pallas kernels for 4% -> 1%
where the time goes in v3:
time: 160 us; the launch traced here: 159 us
  waiting for transfers between devices  60 us (38%)
  starting transfers between devices  32.9 us (21%)
  blocking collectives  24.2 us (15%)
  Pallas kernels  21.2 us (13%)
  matrix products  19.5 us (12%)
    all_to_all x1, waiting for transfers between devices, local(): lax.all_to_all(packed.reshape(PEERS, PEER_ROWS, LANES), PLANE, split_axis...  37.1 us
    all_to_all x1, blocking collectives, local(): lax.all_to_all(gram_rows, ALL, split_axis=0, concat_axis=0, tiled=True)  24.2 us
    dot_general x1, matrix products, local(): jnp.dot(flat, flat.T, precision=lax.Precision.HIGHEST, preferred_element_...  19.5 us
    all_to_all x1, starting transfers between devices, local(): lax.all_to_all(packed.reshape(PEERS, PEER_ROWS, LANES), PLANE, split_axis...  10.7 us
    ppermute x3, starting transfers between devices, local(): lax.ppermute(part, 'sxq', [(i, (i + k) % QUADS) for i in range(QUADS)])  9.67 us
    pallas_call x1, Pallas kernels, local(): pl.pallas_call(pack_kernel, out_shape=jax.ShapeDtypeStruct((PEERS * PEER_...  8.93 us
    ppermute x3, waiting for transfers between devices, local(): lax.ppermute(part, 'sxq', [(i, (i + k) % QUADS) for i in range(QUADS)])  6.5 us
    pallas_call x2, Pallas kernels, deposit(): pl.pallas_call(functools.partial(deposit_kernel, ahead), out_shape=[jax.S...  5.89 us
  transfers between devices with their start and end apart: 10, of which 10 were waited for; matrix products, arithmetic and copies ran while one was open for 12% of the time, Pallas kernels for 1%

profile of v3, /device:TPU:1, one launch (start us, length us, event | category | flops | bytes accessed | tf_op | source)
XLA Modules:
  0.0 159.4 jit_solution(16261585146961934002)
XLA Ops:
  0.6 8.9 %pack.1 = f32[8704,128]{1,0:T(8,128)} custom-call(s32[1]{0:T(128)} %bitcast.1.shift_ref, s32[1,4096]{1,0:T(1,128)} %bitcast.18, s32[1,4096]{1,0:T(1,128)} %bitcast.19, f32[4096,128]{1,0:T(8,128)} %blocks_hbm.1), custom_call_target="tpu_custom_call" | custom-call | tf_op jit(solution)/shard_map/pack/pallas_call | solution.py:352
  9.6 0.0 copy-start
  9.6 10.7 %all-to-all-start = ((f32[64,136,128]{2,1,0:T(8,128)}), f32[64,136,128]{2,1,0:T(8,128)}, u32[]{:S(2)}, u32[]{:S(2)}) async-start(f32[64,136,128]{2,1,0:T(8,128)} %bitcast.17), calls=%async_computation | async-start | bytes 8912896 | tf_op jit(solution)/shard_map/exchange/all_to_all | solution.py:375
  20.3 19.5 %fusion.2 = f32[56,56]{1,0:T(8,128)S(1)} fusion(f32[56,16,16,128]{3,2,1,0:T(8,128)} %past.1), kind=kOutput, calls=%fused_computation.2 | convolution fusion | flops 1233125376 | bytes 7352576 | tf_op jit(solution)/shard_map/history/dot_general | solution.py:382
  39.8 37.1 %all-to-all-done.block_ref.label_ref = f32[64,136,128]{2,1,0:T(8,128)} async-done(((f32[64,136,128]{2,1,0:T(8,128)}), f32[64,136,128]{2,1,0:T(8,128)}, u32[]{:S(2)}, u32[]{:S(2)}) %all-to-all-start) | async-done | bytes 4456480 | tf_op jit(solution)/shard_map/exchange/all_to_all | solution.py:375
  76.9 4.0 %deposit.3 = (f32[256,128]{1,0:T(8,128)S(1)}, f32[256,128]{1,0:T(8,128)S(1)}, f32[256,128]{1,0:T(8,128)S(1)}) custom-call(s32[1]{0:T(128)} %bitcast.quad_ref, f32[64,136,128]{2,1,0:T(8,128)} %all-to-all-done.block_ref.label_ref, f32[64,136,128]{2,1,0:T(8,128)} %all-to-all-done.block_ref.label_ref, f32[128,128]{1,0:T(8,128)S(1)} %copy-done), custom_call_target="tpu_custom_call" | custom-call | tf_op jit(solution)/shard_map/deposit/pallas_call | solution.py:393
  80.9 6.1 %collective-permute-start = (f32[256,128]{1,0:T(8,128)S(1)}, f32[256,128]{1,0:T(8,128)S(1)}, u32[]{:S(2)}, u32[]{:S(2)}) collective-permute-start(f32[256,128]{1,0:T(8,128)S(1)} %get-tuple-element.22), channel_id=1, source_target_pairs={{0,32},{16,48},{32,0},{48,16},{1,33},{17,49},{33,1},{49,17},{2,34}... | collective-permute-start | bytes 393224 | tf_op jit(solution)/shard_map/deposit/ppermute | solution.py:413
  87.0 1.2 collective-permute-start.1
  88.2 2.4 %collective-permute-start.2 = (f32[256,128]{1,0:T(8,128)S(1)}, f32[256,128]{1,0:T(8,128)S(1)}, u32[]{:S(2)}, u32[]{:S(2)}) collective-permute-start(f32[256,128]{1,0:T(8,128)S(1)} %get-tuple-element.24), channel_id=1, source_target_pairs={{0,48},{16,0},{32,16},{48,32},{1,49},{17,1},{33,17},{49,33},{2,50}... | collective-permute-start | bytes 393224 | tf_op jit(solution)/shard_map/deposit/ppermute | solution.py:413
  90.6 1.9 %deposit.2.refs_0_ = f32[256,128]{1,0:T(8,128)S(1)} custom-call(s32[1]{0:T(128)} %bitcast.quad_ref, f32[64,136,128]{2,1,0:T(8,128)} %all-to-all-done.block_ref.label_ref, f32[64,136,128]{2,1,0:T(8,128)} %all-to-all-done.block_ref.label_ref, f32[128,128]{1,0:T(8,128)S(1)} %copy-done), custom_call_target="tpu_custom_call" | custom-call | tf_op jit(solution)/shard_map/deposit/pallas_call | solution.py:393
  92.5 0.6 collective-permute-done.refs_1_
  93.1 4.6 %collective-permute-done.1.refs_2_ = f32[256,128]{1,0:T(8,128)S(1)} collective-permute-done((f32[256,128]{1,0:T(8,128)S(1)}, f32[256,128]{1,0:T(8,128)S(1)}, u32[]{:S(2)}, u32[]{:S(2)}) %collective-permute-start.1) | collective-permute-done | bytes 131104 | tf_op jit(solution)/shard_map/deposit/ppermute | solution.py:413
  97.7 1.3 collective-permute-done.2.refs_3_
  99.0 0.1 halo.3
  99.0 2.3 %collective-permute-start.3 = (f32[3,8,16,128]{3,2,1,0:T(8,128)S(1)}, f32[3,8,16,128]{3,2,1,0:T(8,128)S(1)}, u32[]{:S(2)}, u32[]{:S(2)}) collective-permute-start(f32[3,8,16,128]{3,2,1,0:T(8,128)S(1)} %get-tuple-element.25), channel_id=1, source_target_pairs={{0,8},{8,16},{16,24},{24,32},{32,40},{40,48},{48,56},{1,9},{9,17},... | collective-permute-start | bytes 589832 | tf_op jit(solution)/shard_map/halo/ppermute | solution.py:317
  101.3 1.3 collective-permute-start.4
  102.6 2.6 %collective-permute-done.3.up_ref = f32[3,8,16,128]{3,2,1,0:T(8,128)S(1)} collective-permute-done((f32[3,8,16,128]{3,2,1,0:T(8,128)S(1)}, f32[3,8,16,128]{3,2,1,0:T(8,128)S(1)}, u32[]{:S(2)}, u32[]{:S(2)}) %collective-permute-start.3) | collective-permute-done | bytes 196640 | tf_op jit(solution)/shard_map/halo/ppermute | solution.py:317
  105.2 3.8 %collective-permute-done.4.down_ref = f32[3,8,16,128]{3,2,1,0:T(8,128)S(1)} collective-permute-done((f32[3,8,16,128]{3,2,1,0:T(8,128)S(1)}, f32[3,8,16,128]{3,2,1,0:T(8,128)S(1)}, u32[]{:S(2)}, u32[]{:S(2)}) %collective-permute-start.4) | collective-permute-done | bytes 196640 | tf_op jit(solution)/shard_map/halo/ppermute | solution.py:318
  109.0 0.1 halo.4
  109.0 1.9 %collective-permute-start.5 = (f32[3,32,8,128]{3,2,1,0:T(8,128)S(1)}, f32[3,32,8,128]{3,2,1,0:T(8,128)S(1)}, u32[]{:S(2)}, u32[]{:S(2)}) collective-permute-start(f32[3,32,8,128]{3,2,1,0:T(8,128)S(1)} %get-tuple-element.28), channel_id=1, source_target_pairs={{0,1},{1,2},{2,3},{3,4},{4,5},{5,6},{6,7},{8,9},{9,10},{10,11},{11... | collective-permute-start | bytes 1179656 | tf_op jit(solution)/shard_map/halo/ppermute | solution.py:321
  110.9 3.1 %collective-permute-start.6 = (f32[3,32,8,128]{3,2,1,0:T(8,128)S(1)}, f32[3,32,8,128]{3,2,1,0:T(8,128)S(1)}, u32[]{:S(2)}, u32[]{:S(2)}) collective-permute-start(f32[3,32,8,128]{3,2,1,0:T(8,128)S(1)} %get-tuple-element.29), channel_id=1, source_target_pairs={{1,0},{2,1},{3,2},{4,3},{5,4},{6,5},{7,6},{9,8},{10,9},{11,10},{12... | collective-permute-start | bytes 1179656 | tf_op jit(solution)/shard_map/halo/ppermute | solution.py:322
  114.0 1.6 %collective-permute-done.5.left_ref = f32[3,32,8,128]{3,2,1,0:T(8,128)S(1)} collective-permute-done((f32[3,32,8,128]{3,2,1,0:T(8,128)S(1)}, f32[3,32,8,128]{3,2,1,0:T(8,128)S(1)}, u32[]{:S(2)}, u32[]{:S(2)}) %collective-permute-start.5) | collective-permute-done | bytes 393248 | tf_op jit(solution)/shard_map/halo/ppermute | solution.py:321
  115.6 4.4 %collective-permute-done.6.right_ref = f32[3,32,8,128]{3,2,1,0:T(8,128)S(1)} collective-permute-done((f32[3,32,8,128]{3,2,1,0:T(8,128)S(1)}, f32[3,32,8,128]{3,2,1,0:T(8,128)S(1)}, u32[]{:S(2)}, u32[]{:S(2)}) %collective-permute-start.6) | collective-permute-done | bytes 393248 | tf_op jit(solution)/shard_map/halo/ppermute | solution.py:322
  120.0 0.5 halo.5
  120.5 2.7 %collective-permute-start.7 = (f32[3,8,1024]{2,1,0:T(8,128)S(1)}, f32[3,8,1024]{2,1,0:T(8,128)S(1)}, u32[]{:S(2)}, u32[]{:S(2)}) collective-permute-start(f32[3,8,1024]{2,1,0:T(8,128)S(1)} %get-tuple-element.31), channel_id=1, source_target_pairs={{0,64},{64,128},{128,192},{1,65},{65,129},{129,193},{2,66},{66,130... | collective-permute-start | bytes 294920 | tf_op jit(solution)/shard_map/halo/ppermute | solution.py:327
  123.2 1.3 collective-permute-start.8
  124.5 0.3 collective-permute-done.7.before_ref
  124.8 3.7 %collective-permute-done.8.after_ref = f32[3,8,1024]{2,1,0:T(8,128)S(1)} collective-permute-done((f32[3,8,1024]{2,1,0:T(8,128)S(1)}, f32[3,8,1024]{2,1,0:T(8,128)S(1)}, u32[]{:S(2)}, u32[]{:S(2)}) %collective-permute-start.8) | collective-permute-done | bytes 98336 | tf_op jit(solution)/shard_map/halo/ppermute | solution.py:328
  128.6 5.8 %steps.1 = (f32[16,16,128]{2,1,0:T(8,128)}, f32[256,64]{1,0:T(8,128)S(1)}) custom-call(f32[3,1024,128]{2,1,0:T(8,128)S(1)} %get-tuple-element.30.wide_ref, f32[3,8,1024]{2,1,0:T(8,128)S(1)} %collective-permute-done.7.before_ref, f32[3,8,1024]{2,1,0:T(8,128)S(1)} %collective-permute-done.8.after_ref, f32[56,64]{1,0:T(8,128)S(1)} %pad.4.past_gram, ...), custom_call_target="tpu_custom_call" | custom-call | tf_op jit(solution)/shard_map/steps/pallas_call | solution.py:425
  134.4 24.2 %all_to_all.14 = f32[256,1,64]{2,1,0:T(1,128)S(1)} all-to-all(f32[256,1,64]{2,1,0:T(1,128)S(1)} %bitcast.16), channel_id=1, replica_groups=mesh['fluid'=4,'sxq'=4,'sxp'=2,'sy'=8] {'fluid','sxq','sxp','sy'}, dimensions={0} | all-to-all | bytes 131072 | tf_op jit(solution)/shard_map/gram_sum/all_to_all | solution.py:447
  158.6 0.3 reduce_sum.9
  158.9 0.5 multiply_bitcast_fusion
  (11 shorter events, 0.0 us)
Async XLA Ops:
  9.6 67.3 %copy-start = (f32[128,128]{1,0:T(8,128)S(1)}, f32[128,128]{1,0:T(8,128)}, u32[]{:S(2)}) copy-start(f32[128,128]{1,0:T(8,128)} %map_ref.3) | copy-start | bytes 196612
  9.6 67.3 %all-to-all-start = ((f32[64,136,128]{2,1,0:T(8,128)}), f32[64,136,128]{2,1,0:T(8,128)}, u32[]{:S(2)}, u32[]{:S(2)}) async-start(f32[64,136,128]{2,1,0:T(8,128)} %bitcast.17), calls=%async_computation | async-start | bytes 8912896 | tf_op jit(solution)/shard_map/exchange/all_to_all | solution.py:375
  76.9 22.1 %copy-start.1 = (f32[16,16,128]{2,1,0:T(8,128)S(1)}, f32[16,16,128]{2,1,0:T(8,128)}, u32[]{:S(2)}) copy-start(f32[16,16,128]{2,1,0:T(8,128)} %field_ref.1) | copy-start | bytes 393220
  76.9 22.1 %copy-start.2 = (f32[16,16,128]{2,1,0:T(8,128)S(1)}, f32[16,16,128]{2,1,0:T(8,128)}, u32[]{:S(2)}) copy-start(f32[16,16,128]{2,1,0:T(8,128)} %rate_ref.1) | copy-start | bytes 393220
  76.9 51.7 %slice-start = ((s8[7340032]{0:T(1024)(128)(4,1)}), s8[4194304]{0:T(1024)(128)(4,1)S(1)}, s32[]{:S(2)}) async-start(s8[7340032]{0:T(1024)(128)(4,1)} %bitcast.14), calls=%async_computation.2 | async-start | bytes 8388608
  80.9 12.2 %collective-permute-start = (f32[256,128]{1,0:T(8,128)S(1)}, f32[256,128]{1,0:T(8,128)S(1)}, u32[]{:S(2)}, u32[]{:S(2)}) collective-permute-start(f32[256,128]{1,0:T(8,128)S(1)} %get-tuple-element.22), channel_id=1, source_target_pairs={{0,32},{16,48},{32,0},{48,16},{1,33},{17,49},{33,1},{49,17},{2,34}... | collective-permute-start | bytes 393224 | tf_op jit(solution)/shard_map/deposit/ppermute | solution.py:413
  87.0 10.7 %collective-permute-start.1 = (f32[256,128]{1,0:T(8,128)S(1)}, f32[256,128]{1,0:T(8,128)S(1)}, u32[]{:S(2)}, u32[]{:S(2)}) collective-permute-start(f32[256,128]{1,0:T(8,128)S(1)} %get-tuple-element.23), channel_id=1, source_target_pairs={{0,16},{16,32},{32,48},{48,0},{1,17},{17,33},{33,49},{49,1},{2,18}... | collective-permute-start | bytes 393224 | tf_op jit(solution)/shard_map/deposit/ppermute | solution.py:413
  88.2 40.4 %slice-start.1 = ((s8[7340032]{0:T(1024)(128)(4,1)}), s8[3145728]{0:T(1024)(128)(4,1)S(1)}, s32[]{:S(2)}) async-start(s8[7340032]{0:T(1024)(128)(4,1)} %bitcast.14), calls=%async_computation.3 | async-start | bytes 6291456
  88.2 10.8 %collective-permute-start.2 = (f32[256,128]{1,0:T(8,128)S(1)}, f32[256,128]{1,0:T(8,128)S(1)}, u32[]{:S(2)}, u32[]{:S(2)}) collective-permute-start(f32[256,128]{1,0:T(8,128)S(1)} %get-tuple-element.24), channel_id=1, source_target_pairs={{0,48},{16,0},{32,16},{48,32},{1,49},{17,1},{33,17},{49,33},{2,50}... | collective-permute-start | bytes 393224 | tf_op jit(solution)/shard_map/deposit/ppermute | solution.py:413
  99.0 6.1 %collective-permute-start.3 = (f32[3,8,16,128]{3,2,1,0:T(8,128)S(1)}, f32[3,8,16,128]{3,2,1,0:T(8,128)S(1)}, u32[]{:S(2)}, u32[]{:S(2)}) collective-permute-start(f32[3,8,16,128]{3,2,1,0:T(8,128)S(1)} %get-tuple-element.25), channel_id=1, source_target_pairs={{0,8},{8,16},{16,24},{24,32},{32,40},{40,48},{48,56},{1,9},{9,17},... | collective-permute-start | bytes 589832 | tf_op jit(solution)/shard_map/halo/ppermute | solution.py:317
  101.3 7.7 %collective-permute-start.4 = (f32[3,8,16,128]{3,2,1,0:T(8,128)S(1)}, f32[3,8,16,128]{3,2,1,0:T(8,128)S(1)}, u32[]{:S(2)}, u32[]{:S(2)}) collective-permute-start(f32[3,8,16,128]{3,2,1,0:T(8,128)S(1)} %get-tuple-element.27), channel_id=1, source_target_pairs={{8,0},{16,8},{24,16},{32,24},{40,32},{48,40},{56,48},{9,1},{17,9},... | collective-permute-start | bytes 589832 | tf_op jit(solution)/shard_map/halo/ppermute | solution.py:318
  109.0 6.6 %collective-permute-start.5 = (f32[3,32,8,128]{3,2,1,0:T(8,128)S(1)}, f32[3,32,8,128]{3,2,1,0:T(8,128)S(1)}, u32[]{:S(2)}, u32[]{:S(2)}) collective-permute-start(f32[3,32,8,128]{3,2,1,0:T(8,128)S(1)} %get-tuple-element.28), channel_id=1, source_target_pairs={{0,1},{1,2},{2,3},{3,4},{4,5},{5,6},{6,7},{8,9},{9,10},{10,11},{11... | collective-permute-start | bytes 1179656 | tf_op jit(solution)/shard_map/halo/ppermute | solution.py:321
  110.9 9.1 %collective-permute-start.6 = (f32[3,32,8,128]{3,2,1,0:T(8,128)S(1)}, f32[3,32,8,128]{3,2,1,0:T(8,128)S(1)}, u32[]{:S(2)}, u32[]{:S(2)}) collective-permute-start(f32[3,32,8,128]{3,2,1,0:T(8,128)S(1)} %get-tuple-element.29), channel_id=1, source_target_pairs={{1,0},{2,1},{3,2},{4,3},{5,4},{6,5},{7,6},{9,8},{10,9},{11,10},{12... | collective-permute-start | bytes 1179656 | tf_op jit(solution)/shard_map/halo/ppermute | solution.py:322
  120.5 4.3 %collective-permute-start.7 = (f32[3,8,1024]{2,1,0:T(8,128)S(1)}, f32[3,8,1024]{2,1,0:T(8,128)S(1)}, u32[]{:S(2)}, u32[]{:S(2)}) collective-permute-start(f32[3,8,1024]{2,1,0:T(8,128)S(1)} %get-tuple-element.31), channel_id=1, source_target_pairs={{0,64},{64,128},{128,192},{1,65},{65,129},{129,193},{2,66},{66,130... | collective-permute-start | bytes 294920 | tf_op jit(solution)/shard_map/halo/ppermute | solution.py:327
  123.2 5.4 %collective-permute-start.8 = (f32[3,8,1024]{2,1,0:T(8,128)S(1)}, f32[3,8,1024]{2,1,0:T(8,128)S(1)}, u32[]{:S(2)}, u32[]{:S(2)}) collective-permute-start(f32[3,8,1024]{2,1,0:T(8,128)S(1)} %get-tuple-element.32), channel_id=1, source_target_pairs={{64,0},{128,64},{192,128},{65,1},{129,65},{193,129},{66,2},{130,66... | collective-permute-start | bytes 294920 | tf_op jit(solution)/shard_map/halo/ppermute | solution.py:328

commit v4 on v3

--- a/solution.py
+++ b/solution.py
@@ -17,7 +17,8 @@
 LANES = 128
 QUADS = 4
 PEERS = 64
-PEER_ROWS = QUADS * SLOTS + 8
+PEER_ROWS = QUADS * SLOTS + 1
+ORDER = (2, 1, 3, 0)
 CHUNK = 256
 TILE = 16
 WIDE = TILE + 2 * HALO
@@ -33,6 +34,7 @@
 bf16 = jnp.bfloat16
 
 LIMIT = pltpu.CompilerParams(vmem_limit_bytes=32 * 1024 * 1024)
+LOADS = 4
 FULL = pltpu.CompilerParams(vmem_limit_bytes=60 * 1024 * 1024)
 
 
@@ -48,7 +50,7 @@
 
 
 def pack_kernel(
-    shift_ref,
+    mine_ref,
     owner_hbm,
     line_hbm,
     blocks_hbm,
@@ -72,86 +74,106 @@
     rows = lax.broadcasted_iota(jnp.int32, (CHUNK, CHUNK), 0)
     cols = lax.broadcasted_iota(jnp.int32, (CHUNK, CHUNK), 1)
     earlier = jnp.where(rows < cols, 1.0, 0.0).astype(bf16)
-    places = lax.broadcasted_iota(jnp.int32, (LANES, CHUNK), 0)
-    shift = shift_ref[0]
+    spots = lax.broadcasted_iota(jnp.int32, (LANES, CHUNK), 0)
+    peers = lax.broadcasted_iota(jnp.int32, (PEERS, CHUNK), 0)
+    my_quad, my_turn = mine_ref[0] >> 2, mine_ref[0] & 3
     carry = jnp.zeros((CHUNK, 1), f32)
-    labels = jnp.zeros((CHUNK, LANES), f32)
+    labels = jnp.zeros((PEERS, LANES), f32)
     loads[0].wait()
     loads[1].wait()
-    for c in range(0, owner_ref.shape[1], CHUNK):
-        owner = owner_ref[:, c : c + CHUNK]
-        fluid, sx, sy = owner >> 6, (owner >> 3) & 7, owner & 7
-        peer = (fluid * 2 + (sx & 1)) * 8 + sy
-        quad = sx >> 1
-        match = rows == peer * QUADS + quad
-        hit = jnp.where(match, 1.0, 0.0)
-        hit16 = hit.astype(bf16)
-        before = jnp.dot(hit16, earlier, preferred_element_type=f32)
-        rank = jnp.sum(jnp.where(match, before + carry, 0.0), axis=0, keepdims=True)
-        carry = carry + (before[:, CHUNK - 1 :] + hit[:, CHUNK - 1 :])
-        rank = rank.astype(jnp.int32)
-        slot_ref[:, c : c + CHUNK] = peer * PEER_ROWS + quad * SLOTS + rank
-        value = (line_ref[:, c : c + CHUNK] + 1).astype(f32)
-        spread = jnp.where(places == rank + shift, value, 0.0).astype(bf16)
-        labels = labels + dot_nt(hit16, spread)
-    to_smem = pltpu.make_async_copy(slot_ref, slot_smem, sems.at[3])
-    to_smem.start()
+    span = owner_ref.shape[1] // 2
+    copies = []
+    for begin in (0, span):
+        for c in range(begin, begin + span, CHUNK):
+            owner = owner_ref[:, c : c + CHUNK]
+            fluid, sx, sy = owner >> 6, (owner >> 3) & 7, owner & 7
+            peer = (fluid * 2 + (sx & 1)) * 8 + sy
+            ahead = ((sx >> 1) - my_quad) & 3
+            place = jnp.where(ahead == 0, 3, jnp.where(ahead == 1, 1, jnp.where(ahead == 2, 0, 2)))
+            match = rows == peer * QUADS + place
+            hit = jnp.where(match, 1.0, 0.0)
+            hit16 = hit.astype(bf16)
+            before = jnp.dot(hit16, earlier, preferred_element_type=f32)
+            rank = jnp.sum(jnp.where(match, before + carry, 0.0), axis=0, keepdims=True)
+            carry = carry + (before[:, CHUNK - 1 :] + hit[:, CHUNK - 1 :])
+            rank = rank.astype(jnp.int32)
+            slot_ref[:, c : c + CHUNK] = peer * PEER_ROWS + place * SLOTS + rank
+            value = (line_ref[:, c : c + CHUNK] + 1).astype(f32)
+            spot = ((place + my_turn) & 3) * SLOTS + rank
+            spread = jnp.where(spots == spot, value, 0.0).astype(bf16)
+            labels = labels + dot_nt(jnp.where(peers == peer, 1.0, 0.0).astype(bf16), spread)
+        window = slice(begin, begin + span)
+        copies.append(
+            pltpu.make_async_copy(
+                slot_ref.at[:, window], slot_smem.at[:, window], sems.at[3 + begin // span]
+            )
+        )
+        copies[-1].start()
     for g in range(PEERS):
         at = g * PEER_ROWS + QUADS * SLOTS
-        out_ref[at : at + QUADS, :] = labels[QUADS * g : QUADS * (g + 1)]
-    to_smem.wait()
+        out_ref[at : at + 1, :] = labels[g : g + 1]
     loads[2].wait()
-
-    step = 64
-
-    def place(i, _):
-        base = pl.multiple_of(i * step, step)
-        for t in range(step):
-            out_ref[pl.ds(slot_smem[0, base + t], 1), :] = blocks_ref[pl.ds(base + t, 1), :]
-        return 0
-
-    lax.fori_loop(0, blocks_ref.shape[0] // step, place, 0)
-
-
-def quad_step(ahead, step):
-    value = ahead[0]
-    for n in range(1, len(ahead)):
-        value = jnp.where(step == n, ahead[n], value)
-    return value
-
-
-def deposit_kernel(ahead, quad_ref, block_ref, label_ref, map_ref, *out_refs):
-    step = pl.program_id(0)
-    quad = (quad_ref[0] + quad_step(ahead, step)) % QUADS
+    step = 128
+    for n, copy in enumerate(copies):
+        copy.wait()
+
+        def put(i, _):
+            base = pl.multiple_of(n * span + i * step, step)
+            for t in range(step):
+                out_ref[pl.ds(slot_smem[0, base + t], 1), :] = blocks_ref[pl.ds(base + t, 1), :]
+            return 0
+
+        lax.fori_loop(0, span // step, put, 0)
+
+
+def deposit_kernel(places, received_hbm, map_ref, *refs):
+    outs, (values_ref, total_ref, sems) = refs[: len(places)], refs[len(places) :]
+    rows = PEERS * PEER_ROWS // LOADS
+    loads = [
+        pltpu.make_async_copy(
+            received_hbm.at[n * rows : (n + 1) * rows],
+            values_ref.at[n * rows : (n + 1) * rows],
+            sems.at[n],
+        )
+        for n in range(LOADS)
+    ]
+    for load in loads:
+        load.start()
     lines = lax.broadcasted_iota(jnp.int32, (LINES, LANES), 0).astype(f32) + 1.0
-    labels = label_ref[:, pl.ds(quad, 1), :].reshape(PEERS // 4, 4, LANES).sum(axis=1)
-    total = jnp.zeros((LINES, 2 * LANES), f32)
-    for g in range(PEERS // 8):
-        marks = [
-            jnp.where(lines == labels[h : h + 1], 1.0, 0.0).astype(bf16)
-            for h in (2 * g, 2 * g + 1)
-        ]
-        high, low = split(block_ref[8 * g : 8 * g + 8].reshape(8 * SLOTS, LANES))
-        total = total + jnp.dot(
-            jnp.concatenate(marks, axis=1),
-            jnp.concatenate([high, low], axis=1),
-            preferred_element_type=f32,
-        )
-    high, low = split(total[:, :LANES] + total[:, LANES:])
+    group = lax.broadcasted_iota(jnp.int32, (1, LANES), 1) // SLOTS
+
+    def gathered(first, place):
+        label, values = jnp.zeros((1, LANES), f32), [None] * 4
+        for t in range(4):
+            at = (first + t) * PEER_ROWS
+            turn = (place + t) % 4
+            row = values_ref[at + QUADS * SLOTS : at + PEER_ROWS, :]
+            label = jnp.where(group == turn, row, label)
+            values[turn] = values_ref[at + place * SLOTS : at + (place + 1) * SLOTS, :]
+        return jnp.where(lines == label, 1.0, 0.0).astype(bf16), jnp.concatenate(values, axis=0)
+
+    for n, load in enumerate(loads):
+        load.wait()
+        for first in range(n * PEERS // LOADS, (n + 1) * PEERS // LOADS, 8):
+            for k, place in enumerate(places):
+                marks, values = zip(gathered(first, place), gathered(first + 4, place))
+                high, low = split(jnp.concatenate(values, axis=0))
+                part = jnp.dot(
+                    jnp.concatenate(marks, axis=1),
+                    jnp.concatenate([high, low], axis=1),
+                    preferred_element_type=f32,
+                )
+                total_ref[k] = part if first == 0 else total_ref[k] + part
     map_high, map_low = split(map_ref[...])
     both = jnp.concatenate([map_high, map_low], axis=1)
     once = jnp.concatenate([map_high, jnp.zeros_like(map_low)], axis=1)
-    mapped = jnp.dot(
-        jnp.concatenate([high, low], axis=1),
-        jnp.concatenate([both, once], axis=0),
-        preferred_element_type=f32,
-    )
-    result = source_gain * (mapped[:, :LANES] + mapped[:, LANES:])
-    for n, out_ref in enumerate(out_refs):
-
-        @pl.when(step == n)
-        def _():
-            out_ref[...] = result
+    weights = jnp.concatenate([both, once], axis=0)
+    for k, out_ref in enumerate(outs):
+        high, low = split(total_ref[k, :, :LANES] + total_ref[k, :, LANES:])
+        mapped = jnp.dot(
+            jnp.concatenate([high, low], axis=1), weights, preferred_element_type=f32
+        )
+        out_ref[...] = source_gain * (mapped[:, :LANES] + mapped[:, LANES:])
 
 
 def cut_kernel(field_ref, rate_ref, *refs):
@@ -189,6 +211,7 @@
 
 
 def step_kernel(
+    scale,
     wide_ref,
     before_ref,
     after_ref,
@@ -216,24 +239,26 @@
         for k, (to, off) in enumerate(((now_e, pad), (rate_e, 0), (src_e, 0))):
             lanes = jnp.concatenate([after_ref[k, :, own], none, before_ref[k, :, own]], axis=0)
             to[off + r : off + r + LANES, :] = lanes.T
-    lane = lax.broadcasted_iota(jnp.int32, (WIDE, LANES), 1)
-    first, last = lane == 0, lane == LANES - 1
 
     def advance(a_m, a_e, b_m, b_e, s):
+        alone = s == STEPS - 1
+        begin, height = (HALO, TILE) if alone else (0, WIDE)
+        lane = lax.broadcasted_iota(jnp.int32, (height, LANES), 1)
+        first, last = lane == 0, lane == LANES - 1
         for x in range(s + 1, WIDE - 1 - s):
-            r = x * WIDE
-            at = lambda off: pl.ds(r + pad + off, WIDE)
-            own = pl.ds(r, WIDE)
+            r = x * WIDE + begin
+            at = lambda off: pl.ds(r + pad + off, height)
+            own = pl.ds(r, height)
             m, e = a_m[at(0), :], a_e[at(0), :]
             roll = lambda v, d: pltpu.roll(v, d % LANES, 1)
             mr, er, ml, el = roll(m, 1), roll(e, 1), roll(m, -1), roll(e, -1)
-            sides = (
+            sides = [
                 (a_m, b_m, m, jnp.where(first, er, mr) + jnp.where(last, el, ml)),
                 (a_e, b_e, e, jnp.where(first, mr, er) + jnp.where(last, ml, el)),
-            )
+            ]
             rates = (wide_ref[1, own, :], rate_e[own, :])
             sources = (wide_ref[2, own, :], src_e[own, :])
-            for (a, b, v, beside), rate, src in zip(sides, rates, sources):
+            for (a, b, v, beside), rate, src in zip(sides[: 1 if alone else 2], rates, sources):
                 beside = beside + (a[at(-WIDE), :] + a[at(WIDE), :])
                 beside = beside + (a[at(-1), :] + a[at(1), :])
                 b[at(0), :] = v + rate * (beside - 6.0 * v) + src
@@ -278,7 +303,8 @@
     )
     pick = snap_of(tallest, 1) == lax.broadcasted_iota(jnp.int32, tallest, 0)
     low = dot_nt(jnp.where(pick, 1.0, 0.0), products, lax.Precision.HIGHEST)
-    upper = past_gram[...] + right[:HIST]
+    upper = scale * (past_gram[...] + right[:HIST])
+    low = scale * low
     for f in range(rows_ref.shape[0] // SNAPS):
         rows_ref[f * SNAPS : f * SNAPS + HIST, :] = upper
         rows_ref[f * SNAPS + HIST : (f + 1) * SNAPS, :] = low
@@ -329,10 +355,6 @@
     return wide, before, after
 
 
-def whole(shape):
-    return pl.BlockSpec(shape, lambda *_: (0,) * len(shape))
-
-
 def local(
     opening_conductor_warmth,
     cellwise_diffusivity,
@@ -348,7 +370,8 @@
     hbm = pl.BlockSpec(memory_space=pltpu.HBM)
 
     with jax.named_scope("pack"):
-        shift = (lax.axis_index("sy") % 4 * SLOTS).astype(jnp.int32).reshape(1)
+        mine = lax.axis_index("sxq") * 4 + lax.axis_index("sy") % 4
+        mine = mine.astype(jnp.int32).reshape(1)
         packed = pl.pallas_call(
             pack_kernel,
             out_shape=jax.ShapeDtypeStruct((PEERS * PEER_ROWS, LANES), f32),
@@ -360,11 +383,11 @@
                 pltpu.VMEM((blocks, LANES), f32),
                 pltpu.VMEM((1, blocks), jnp.int32),
                 pltpu.SMEM((1, blocks), jnp.int32),
-                pltpu.SemaphoreType.DMA((4,)),
+                pltpu.SemaphoreType.DMA((5,)),
             ],
             compiler_params=FULL,
         )(
-            shift,
+            mine,
             receiving_processor_per_piece.T,
             boundary_line_position_in_tile.T,
             boundary_heat_rate_pieces,
@@ -373,7 +396,7 @@
     with jax.named_scope("exchange"):
         packed, states = lax.optimization_barrier((packed, previous_thermal_states))
         received = lax.all_to_all(
-            packed.reshape(PEERS, PEER_ROWS, LANES), PLANE, split_axis=0, concat_axis=0, tiled=True
+            packed.reshape(PEERS * PEER_ROWS, 1, LANES), PLANE, split_axis=0, concat_axis=0, tiled=True
         )
 
     with jax.named_scope("history"):
@@ -386,34 +409,27 @@
 
     with jax.named_scope("deposit"):
         received, past_gram = lax.optimization_barrier((received, past_gram))
-        mine = lax.axis_index("sxq").astype(jnp.int32).reshape(1)
-
-        def deposit(*ahead):
-            quad_of = lambda step, quad: (quad[0] + quad_step(ahead, step)) % QUADS
+        received = received.reshape(PEERS * PEER_ROWS, LANES)
+
+        def deposit(*places):
             return pl.pallas_call(
-                functools.partial(deposit_kernel, ahead),
-                out_shape=[jax.ShapeDtypeStruct((LINES, LANES), f32)] * len(ahead),
-                grid_spec=pltpu.PrefetchScalarGridSpec(
-                    num_scalar_prefetch=1,
-                    grid=(len(ahead),),
-                    in_specs=[
-                        pl.BlockSpec(
-                            (PEERS, SLOTS, LANES), lambda step, quad: (0, quad_of(step, quad), 0)
-                        ),
-                        pl.BlockSpec((PEERS, 8, LANES), lambda *_: (0, QUADS * SLOTS // 8, 0)),
-                        whole((LANES, LANES)),
-                    ],
-                    out_specs=[whole((LINES, LANES))] * len(ahead),
-                ),
+                functools.partial(deposit_kernel, places),
+                out_shape=[jax.ShapeDtypeStruct((LINES, LANES), f32)] * len(places),
+                in_specs=[hbm, vmem],
+                out_specs=[vmem] * len(places),
+                scratch_shapes=[
+                    pltpu.VMEM((PEERS * PEER_ROWS, LANES), f32),
+                    pltpu.VMEM((len(places), LINES, 2 * LANES), f32),
+                    pltpu.SemaphoreType.DMA((LOADS,)),
+                ],
                 compiler_params=LIMIT,
-            )(mine, received, received, piece_to_solid_line_mapping)
-
-        ahead = (2, 1, 3)
+            )(received, piece_to_solid_line_mapping)
+
         parts = [
             lax.ppermute(part, "sxq", [(i, (i + k) % QUADS) for i in range(QUADS)])
-            for k, part in zip(ahead, deposit(*ahead))
+            for k, part in zip(ORDER, deposit(0, 1, 2))
         ]
-        parts = [*deposit(0), *parts]
+        parts = [*deposit(3), *parts]
 
     with jax.named_scope("halo"):
         wide, before, after = widened(opening_conductor_warmth, cellwise_diffusivity, parts)
@@ -423,7 +439,7 @@
         grid_rows = WIDE * WIDE
         buffer = pltpu.VMEM((grid_rows + 2 * WIDE, LANES), f32)
         field, gram_rows = pl.pallas_call(
-            step_kernel,
+            functools.partial(step_kernel, 1.0 / cells),
             out_shape=(
                 jax.ShapeDtypeStruct((TILE, TILE, LANES), f32),
                 jax.ShapeDtypeStruct((rows, SNAPS), f32),
@@ -445,7 +461,7 @@
 
     with jax.named_scope("gram_sum"):
         shares = lax.all_to_all(gram_rows, ALL, split_axis=0, concat_axis=0, tiled=True)
-        inner_product_matrix = jnp.sum(shares, axis=0, keepdims=True) / cells
+        inner_product_matrix = jnp.sum(shares, axis=0, keepdims=True)
     return field, inner_product_matrix
 
 

time: 160 us -> 156 us (0.975)
  waiting for transfers between devices: 60 us -> 56.7 us
    all_to_all x1, waiting for transfers between devices: 37.1 us -> 34.5 us  [local(): lax.all_to_all(packed.reshape(PEERS * PEER_ROWS, 1, LANES), PLANE, split_...]
  transfers between devices with their start and end apart: 10 -> 10, of which waited for: 10 -> 10; matrix products, arithmetic and copies ran while one was open for 12% -> 13% of each run, Pallas kernels for 1% -> 2%
where the time goes in v4:
time: 156 us
  waiting for transfers between devices  56.7 us (36%)
  starting transfers between devices  32.6 us (21%)
  blocking collectives  24.9 us (16%)
  Pallas kernels  20.3 us (13%)
  matrix products  19.5 us (12%)
    all_to_all x1, waiting for transfers between devices, local(): lax.all_to_all(packed.reshape(PEERS * PEER_ROWS, 1, LANES), PLANE, split_...  34.5 us
    all_to_all x1, blocking collectives, local(): lax.all_to_all(gram_rows, ALL, split_axis=0, concat_axis=0, tiled=True)  24.9 us
    dot_general x1, matrix products, local(): jnp.dot(flat, flat.T, precision=lax.Precision.HIGHEST, preferred_element_...  19.5 us
    all_to_all x1, starting transfers between devices, local(): lax.all_to_all(packed.reshape(PEERS * PEER_ROWS, 1, LANES), PLANE, split_...  10.7 us
    ppermute x3, starting transfers between devices, local(): lax.ppermute(part, 'sxq', [(i, (i + k) % QUADS) for i in range(QUADS)])  9.68 us
    pallas_call x1, Pallas kernels, local(): pl.pallas_call(pack_kernel, out_shape=jax.ShapeDtypeStruct((PEERS * PEER_...  8.25 us
    pallas_call x1, Pallas kernels, local(): pl.pallas_call(functools.partial(step_kernel, 1.0 / cells), out_shape=(ja...  5.81 us
    pallas_call x2, Pallas kernels, deposit(): pl.pallas_call(functools.partial(deposit_kernel, places), out_shape=[jax....  5.69 us
  transfers between devices with their start and end apart: 10, of which 10 were waited for; matrix products, arithmetic and copies ran while one was open for 13% of the time, Pallas kernels for 2%

profile of v4, /device:TPU:1, one launch (start us, length us, event | category | flops | bytes accessed | tf_op | source)
XLA Modules:
  0.0 155.6 jit_solution(14799361111100237522)
XLA Ops:
  0.6 8.2 %pack.1 = f32[8256,128]{1,0:T(8,128)} custom-call(s32[1]{0:T(128)} %bitcast.mine_ref, s32[1,4096]{1,0:T(1,128)} %bitcast.19, s32[1,4096]{1,0:T(1,128)} %bitcast.20, f32[4096,128]{1,0:T(8,128)} %blocks_hbm.1), custom_call_target="tpu_custom_call" | custom-call | tf_op jit(solution)/shard_map/pack/pallas_call | solution.py:375
  8.9 0.0 copy-start
  8.9 10.7 %all-to-all-start = ((f32[8256,1,128]{2,1,0:T(1,128)}), f32[8256,1,128]{2,1,0:T(1,128)}, u32[]{:S(2)}, u32[]{:S(2)}) async-start(f32[8256,1,128]{2,1,0:T(1,128)} %bitcast.18), calls=%async_computation | async-start | bytes 8454144 | tf_op jit(solution)/shard_map/exchange/all_to_all | solution.py:398
  19.6 0.0 slice-start
  19.6 19.5 %fusion.2 = f32[56,56]{1,0:T(8,128)S(1)} fusion(f32[56,16,16,128]{3,2,1,0:T(8,128)} %past.1), kind=kOutput, calls=%fused_computation.2 | convolution fusion | flops 1233125376 | bytes 7352576 | tf_op jit(solution)/shard_map/history/dot_general | solution.py:405
  39.1 34.5 %all-to-all-done = f32[8256,1,128]{2,1,0:T(1,128)} async-done(((f32[8256,1,128]{2,1,0:T(1,128)}), f32[8256,1,128]{2,1,0:T(1,128)}, u32[]{:S(2)}, u32[]{:S(2)}) %all-to-all-start) | async-done | bytes 4227104 | tf_op jit(solution)/shard_map/exchange/all_to_all | solution.py:398
  73.6 3.1 %deposit.3 = (f32[256,128]{1,0:T(8,128)S(1)}, f32[256,128]{1,0:T(8,128)S(1)}, f32[256,128]{1,0:T(8,128)S(1)}) custom-call(f32[8256,128]{1,0:T(8,128)} %bitcast.7.received_hbm, f32[128,128]{1,0:T(8,128)S(1)} %copy-done), custom_call_target="tpu_custom_call" | custom-call | tf_op jit(solution)/shard_map/deposit/pallas_call | solution.py:415
  76.7 6.1 %collective-permute-start = (f32[256,128]{1,0:T(8,128)S(1)}, f32[256,128]{1,0:T(8,128)S(1)}, u32[]{:S(2)}, u32[]{:S(2)}) collective-permute-start(f32[256,128]{1,0:T(8,128)S(1)} %get-tuple-element.22), channel_id=1, source_target_pairs={{0,32},{16,48},{32,0},{48,16},{1,33},{17,49},{33,1},{49,17},{2,34}... | collective-permute-start | bytes 393224 | tf_op jit(solution)/shard_map/deposit/ppermute | solution.py:429
  82.8 1.2 collective-permute-start.1
  84.0 2.4 %collective-permute-start.2 = (f32[256,128]{1,0:T(8,128)S(1)}, f32[256,128]{1,0:T(8,128)S(1)}, u32[]{:S(2)}, u32[]{:S(2)}) collective-permute-start(f32[256,128]{1,0:T(8,128)S(1)} %get-tuple-element.24), channel_id=1, source_target_pairs={{0,48},{16,0},{32,16},{48,32},{1,49},{17,1},{33,17},{49,33},{2,50}... | collective-permute-start | bytes 393224 | tf_op jit(solution)/shard_map/deposit/ppermute | solution.py:429
  86.4 2.6 %deposit.2.refs_0_ = f32[256,128]{1,0:T(8,128)S(1)} custom-call(f32[8256,128]{1,0:T(8,128)} %bitcast.7.received_hbm, f32[128,128]{1,0:T(8,128)S(1)} %copy-done), custom_call_target="tpu_custom_call" | custom-call | tf_op jit(solution)/shard_map/deposit/pallas_call | solution.py:415
  89.0 0.2 collective-permute-done.refs_1_
  89.2 4.3 %collective-permute-done.1.refs_2_ = f32[256,128]{1,0:T(8,128)S(1)} collective-permute-done((f32[256,128]{1,0:T(8,128)S(1)}, f32[256,128]{1,0:T(8,128)S(1)}, u32[]{:S(2)}, u32[]{:S(2)}) %collective-permute-start.1) | collective-permute-done | bytes 131104 | tf_op jit(solution)/shard_map/deposit/ppermute | solution.py:429
  93.5 1.0 collective-permute-done.2.refs_3_
  94.6 0.1 halo.3
  94.6 2.6 %collective-permute-start.3 = (f32[3,8,16,128]{3,2,1,0:T(8,128)S(1)}, f32[3,8,16,128]{3,2,1,0:T(8,128)S(1)}, u32[]{:S(2)}, u32[]{:S(2)}) collective-permute-start(f32[3,8,16,128]{3,2,1,0:T(8,128)S(1)} %get-tuple-element.25), channel_id=1, source_target_pairs={{0,8},{8,16},{16,24},{24,32},{32,40},{40,48},{48,56},{1,9},{9,17},... | collective-permute-start | bytes 589832 | tf_op jit(solution)/shard_map/halo/ppermute | solution.py:343
  97.2 1.3 collective-permute-start.4
  98.5 2.6 %collective-permute-done.3.up_ref = f32[3,8,16,128]{3,2,1,0:T(8,128)S(1)} collective-permute-done((f32[3,8,16,128]{3,2,1,0:T(8,128)S(1)}, f32[3,8,16,128]{3,2,1,0:T(8,128)S(1)}, u32[]{:S(2)}, u32[]{:S(2)}) %collective-permute-start.3) | collective-permute-done | bytes 196640 | tf_op jit(solution)/shard_map/halo/ppermute | solution.py:343
  101.1 3.8 %collective-permute-done.4.down_ref = f32[3,8,16,128]{3,2,1,0:T(8,128)S(1)} collective-permute-done((f32[3,8,16,128]{3,2,1,0:T(8,128)S(1)}, f32[3,8,16,128]{3,2,1,0:T(8,128)S(1)}, u32[]{:S(2)}, u32[]{:S(2)}) %collective-permute-start.4) | collective-permute-done | bytes 196640 | tf_op jit(solution)/shard_map/halo/ppermute | solution.py:344
  104.9 0.1 halo.4
  105.0 1.9 %collective-permute-start.5 = (f32[3,32,8,128]{3,2,1,0:T(8,128)S(1)}, f32[3,32,8,128]{3,2,1,0:T(8,128)S(1)}, u32[]{:S(2)}, u32[]{:S(2)}) collective-permute-start(f32[3,32,8,128]{3,2,1,0:T(8,128)S(1)} %get-tuple-element.28), channel_id=1, source_target_pairs={{0,1},{1,2},{2,3},{3,4},{4,5},{5,6},{6,7},{8,9},{9,10},{10,11},{11... | collective-permute-start | bytes 1179656 | tf_op jit(solution)/shard_map/halo/ppermute | solution.py:347
  106.9 2.9 %collective-permute-start.6 = (f32[3,32,8,128]{3,2,1,0:T(8,128)S(1)}, f32[3,32,8,128]{3,2,1,0:T(8,128)S(1)}, u32[]{:S(2)}, u32[]{:S(2)}) collective-permute-start(f32[3,32,8,128]{3,2,1,0:T(8,128)S(1)} %get-tuple-element.29), channel_id=1, source_target_pairs={{1,0},{2,1},{3,2},{4,3},{5,4},{6,5},{7,6},{9,8},{10,9},{11,10},{12... | collective-permute-start | bytes 1179656 | tf_op jit(solution)/shard_map/halo/ppermute | solution.py:348
  109.8 1.8 %collective-permute-done.5.left_ref = f32[3,32,8,128]{3,2,1,0:T(8,128)S(1)} collective-permute-done((f32[3,32,8,128]{3,2,1,0:T(8,128)S(1)}, f32[3,32,8,128]{3,2,1,0:T(8,128)S(1)}, u32[]{:S(2)}, u32[]{:S(2)}) %collective-permute-start.5) | collective-permute-done | bytes 393248 | tf_op jit(solution)/shard_map/halo/ppermute | solution.py:347
  111.6 4.4 %collective-permute-done.6.right_ref = f32[3,32,8,128]{3,2,1,0:T(8,128)S(1)} collective-permute-done((f32[3,32,8,128]{3,2,1,0:T(8,128)S(1)}, f32[3,32,8,128]{3,2,1,0:T(8,128)S(1)}, u32[]{:S(2)}, u32[]{:S(2)}) %collective-permute-start.6) | collective-permute-done | bytes 393248 | tf_op jit(solution)/shard_map/halo/ppermute | solution.py:348
  116.0 0.5 halo.5
  116.5 2.3 %collective-permute-start.7 = (f32[3,8,1024]{2,1,0:T(8,128)S(1)}, f32[3,8,1024]{2,1,0:T(8,128)S(1)}, u32[]{:S(2)}, u32[]{:S(2)}) collective-permute-start(f32[3,8,1024]{2,1,0:T(8,128)S(1)} %get-tuple-element.31), channel_id=1, source_target_pairs={{0,64},{64,128},{128,192},{1,65},{65,129},{129,193},{2,66},{66,130... | collective-permute-start | bytes 294920 | tf_op jit(solution)/shard_map/halo/ppermute | solution.py:353
  118.8 1.3 collective-permute-start.8
  120.1 0.3 collective-permute-done.7.before_ref
  120.4 3.7 %collective-permute-done.8.after_ref = f32[3,8,1024]{2,1,0:T(8,128)S(1)} collective-permute-done((f32[3,8,1024]{2,1,0:T(8,128)S(1)}, f32[3,8,1024]{2,1,0:T(8,128)S(1)}, u32[]{:S(2)}, u32[]{:S(2)}) %collective-permute-start.8) | collective-permute-done | bytes 98336 | tf_op jit(solution)/shard_map/halo/ppermute | solution.py:354
  124.1 5.8 %steps.1 = (f32[16,16,128]{2,1,0:T(8,128)}, f32[256,64]{1,0:T(8,128)S(1)}) custom-call(f32[3,1024,128]{2,1,0:T(8,128)S(1)} %get-tuple-element.30.wide_ref, f32[3,8,1024]{2,1,0:T(8,128)S(1)} %collective-permute-done.7.before_ref, f32[3,8,1024]{2,1,0:T(8,128)S(1)} %collective-permute-done.8.after_ref, f32[56,64]{1,0:T(8,128)S(1)} %pad.4.past_gram, ...), custom_call_target="tpu_custom_call" | custom-call | tf_op jit(solution)/shard_map/steps/pallas_call | solution.py:441
  129.9 24.9 %all_to_all.14 = f32[256,1,64]{2,1,0:T(1,128)S(1)} all-to-all(f32[256,1,64]{2,1,0:T(1,128)S(1)} %bitcast.17), channel_id=1, replica_groups=mesh['fluid'=4,'sxq'=4,'sxp'=2,'sy'=8] {'fluid','sxq','sxp','sy'}, dimensions={0} | all-to-all | bytes 131072 | tf_op jit(solution)/shard_map/gram_sum/all_to_all | solution.py:463
  154.8 0.8 reduce_sum.9
  (10 shorter events, 0.0 us)
Async XLA Ops:
  8.9 64.7 %copy-start = (f32[128,128]{1,0:T(8,128)S(1)}, f32[128,128]{1,0:T(8,128)}, u32[]{:S(2)}) copy-start(f32[128,128]{1,0:T(8,128)} %map_ref.3) | copy-start | bytes 196612
  8.9 64.7 %all-to-all-start = ((f32[8256,1,128]{2,1,0:T(1,128)}), f32[8256,1,128]{2,1,0:T(1,128)}, u32[]{:S(2)}, u32[]{:S(2)}) async-start(f32[8256,1,128]{2,1,0:T(1,128)} %bitcast.18), calls=%async_computation | async-start | bytes 8454144 | tf_op jit(solution)/shard_map/exchange/all_to_all | solution.py:398
  19.6 75.0 %copy-start.1 = (f32[16,16,128]{2,1,0:T(8,128)S(1)}, f32[16,16,128]{2,1,0:T(8,128)}, u32[]{:S(2)}) copy-start(f32[16,16,128]{2,1,0:T(8,128)} %field_ref.1) | copy-start | bytes 393220
  19.6 75.0 %copy-start.2 = (f32[16,16,128]{2,1,0:T(8,128)S(1)}, f32[16,16,128]{2,1,0:T(8,128)}, u32[]{:S(2)}) copy-start(f32[16,16,128]{2,1,0:T(8,128)} %rate_ref.1) | copy-start | bytes 393220
  19.6 104.5 %slice-start = ((s8[7340032]{0:T(1024)(128)(4,1)}), s8[3145728]{0:T(1024)(128)(4,1)S(1)}, s32[]{:S(2)}) async-start(s8[7340032]{0:T(1024)(128)(4,1)} %bitcast.15), calls=%async_computation.2 | async-start | bytes 6291456
  73.6 50.5 %slice-start.1 = ((s8[7340032]{0:T(1024)(128)(4,1)}), s8[4194304]{0:T(1024)(128)(4,1)S(1)}, s32[]{:S(2)}) async-start(s8[7340032]{0:T(1024)(128)(4,1)} %bitcast.15), calls=%async_computation.3 | async-start | bytes 8388608
  76.7 12.5 %collective-permute-start = (f32[256,128]{1,0:T(8,128)S(1)}, f32[256,128]{1,0:T(8,128)S(1)}, u32[]{:S(2)}, u32[]{:S(2)}) collective-permute-start(f32[256,128]{1,0:T(8,128)S(1)} %get-tuple-element.22), channel_id=1, source_target_pairs={{0,32},{16,48},{32,0},{48,16},{1,33},{17,49},{33,1},{49,17},{2,34}... | collective-permute-start | bytes 393224 | tf_op jit(solution)/shard_map/deposit/ppermute | solution.py:429
  82.8 10.8 %collective-permute-start.1 = (f32[256,128]{1,0:T(8,128)S(1)}, f32[256,128]{1,0:T(8,128)S(1)}, u32[]{:S(2)}, u32[]{:S(2)}) collective-permute-start(f32[256,128]{1,0:T(8,128)S(1)} %get-tuple-element.23), channel_id=1, source_target_pairs={{0,16},{16,32},{32,48},{48,0},{1,17},{17,33},{33,49},{49,1},{2,18}... | collective-permute-start | bytes 393224 | tf_op jit(solution)/shard_map/deposit/ppermute | solution.py:429
  84.0 10.6 %collective-permute-start.2 = (f32[256,128]{1,0:T(8,128)S(1)}, f32[256,128]{1,0:T(8,128)S(1)}, u32[]{:S(2)}, u32[]{:S(2)}) collective-permute-start(f32[256,128]{1,0:T(8,128)S(1)} %get-tuple-element.24), channel_id=1, source_target_pairs={{0,48},{16,0},{32,16},{48,32},{1,49},{17,1},{33,17},{49,33},{2,50}... | collective-permute-start | bytes 393224 | tf_op jit(solution)/shard_map/deposit/ppermute | solution.py:429
  94.6 6.5 %collective-permute-start.3 = (f32[3,8,16,128]{3,2,1,0:T(8,128)S(1)}, f32[3,8,16,128]{3,2,1,0:T(8,128)S(1)}, u32[]{:S(2)}, u32[]{:S(2)}) collective-permute-start(f32[3,8,16,128]{3,2,1,0:T(8,128)S(1)} %get-tuple-element.25), channel_id=1, source_target_pairs={{0,8},{8,16},{16,24},{24,32},{32,40},{40,48},{48,56},{1,9},{9,17},... | collective-permute-start | bytes 589832 | tf_op jit(solution)/shard_map/halo/ppermute | solution.py:343
  97.2 7.7 %collective-permute-start.4 = (f32[3,8,16,128]{3,2,1,0:T(8,128)S(1)}, f32[3,8,16,128]{3,2,1,0:T(8,128)S(1)}, u32[]{:S(2)}, u32[]{:S(2)}) collective-permute-start(f32[3,8,16,128]{3,2,1,0:T(8,128)S(1)} %get-tuple-element.27), channel_id=1, source_target_pairs={{8,0},{16,8},{24,16},{32,24},{40,32},{48,40},{56,48},{9,1},{17,9},... | collective-permute-start | bytes 589832 | tf_op jit(solution)/shard_map/halo/ppermute | solution.py:344
  105.0 6.6 %collective-permute-start.5 = (f32[3,32,8,128]{3,2,1,0:T(8,128)S(1)}, f32[3,32,8,128]{3,2,1,0:T(8,128)S(1)}, u32[]{:S(2)}, u32[]{:S(2)}) collective-permute-start(f32[3,32,8,128]{3,2,1,0:T(8,128)S(1)} %get-tuple-element.28), channel_id=1, source_target_pairs={{0,1},{1,2},{2,3},{3,4},{4,5},{5,6},{6,7},{8,9},{9,10},{10,11},{11... | collective-permute-start | bytes 1179656 | tf_op jit(solution)/shard_map/halo/ppermute | solution.py:347
  106.9 9.1 %collective-permute-start.6 = (f32[3,32,8,128]{3,2,1,0:T(8,128)S(1)}, f32[3,32,8,128]{3,2,1,0:T(8,128)S(1)}, u32[]{:S(2)}, u32[]{:S(2)}) collective-permute-start(f32[3,32,8,128]{3,2,1,0:T(8,128)S(1)} %get-tuple-element.29), channel_id=1, source_target_pairs={{1,0},{2,1},{3,2},{4,3},{5,4},{6,5},{7,6},{9,8},{10,9},{11,10},{12... | collective-permute-start | bytes 1179656 | tf_op jit(solution)/shard_map/halo/ppermute | solution.py:348
  116.5 3.9 %collective-permute-start.7 = (f32[3,8,1024]{2,1,0:T(8,128)S(1)}, f32[3,8,1024]{2,1,0:T(8,128)S(1)}, u32[]{:S(2)}, u32[]{:S(2)}) collective-permute-start(f32[3,8,1024]{2,1,0:T(8,128)S(1)} %get-tuple-element.31), channel_id=1, source_target_pairs={{0,64},{64,128},{128,192},{1,65},{65,129},{129,193},{2,66},{66,130... | collective-permute-start | bytes 294920 | tf_op jit(solution)/shard_map/halo/ppermute | solution.py:353
  118.8 5.4 %collective-permute-start.8 = (f32[3,8,1024]{2,1,0:T(8,128)S(1)}, f32[3,8,1024]{2,1,0:T(8,128)S(1)}, u32[]{:S(2)}, u32[]{:S(2)}) collective-permute-start(f32[3,8,1024]{2,1,0:T(8,128)S(1)} %get-tuple-element.32), channel_id=1, source_target_pairs={{64,0},{128,64},{192,128},{65,1},{129,65},{193,129},{66,2},{130,66... | collective-permute-start | bytes 294920 | tf_op jit(solution)/shard_map/halo/ppermute | solution.py:354
